TPU v7x, 512 devices: a whole 4x8x8 slice. The times are simulated.
512 devices in a mesh: slab: 64 (over z, y_lo, core), grp: 8 (over y_hi, x).
Axes of the slice: x: 4, y: 8 (y_hi: 2, y_lo: 4; y = y_hi * 4 + y_lo), z: 8, core: 2. Of those that a mesh axis runs over, the one named last changes fastest.
Arguments:
- sound_speed: float32 [64, 256, 256], P('slab'), may hold values from 0.5 to 1
- density: float32 [64, 256, 256], P('slab'), may hold values from 0.7 to 1.4
- attenuation: float32 [64, 256, 256], P('slab'), may hold values from 0.01 to 0.2
- wavelet: float32 [4], replicated, may hold values from -4 to 4
- weights: bfloat16 [8, 1024], replicated, may hold values from -4 to 4
- emitter_group: int32 [1024], replicated, may hold values from 0 to 7
- emitter_cell: int32 [1024], replicated, may hold values from 0 to 4194303, as said below
- receiver_cell: int32 [8192], P('slab'), may hold values from 0 to 65535, as said below
- pressure_start: float32 [8, 64, 256, 256], P('grp', 'slab'), may hold values from -6 to 6
- velocity_start: float32 [3, 8, 64, 256, 256], P(None, 'grp', 'slab'), may hold values from -3 to 3
- observed: bfloat16 [1024, 4, 8192], P('grp', None, 'slab'), may hold values from -0.59765625 to 0.59765625
Outputs:
- grad_speed: float32 [64, 256, 256], P('slab', 'grp')
- grad_atten: float32 [64, 256, 256], P('slab', 'grp')
Inputs may be any that keep to these rules, and one draw needn't show every extreme that they name: `emitter_cell`: each emitter sits at the cell of some receiver (the transducers both emit and record); several emitters may share a cell. `receiver_cell`: cells are counted within the 1 x 256 x 256 block of the receiver's own slab, z slowest and y fastest; several receivers may share a cell. `emitter_group`: the group of encoded sources that an emitter takes part in.
All inputs are finite; a program needn't handle non-finite values.
Results may differ from a plain program's by a relative error of at most 0.0003.
Values may be sent and summed in bfloat16 or wider, within the bound.
A program may use at most 64 MiB of HBM per device.

v0:
```python
import jax
import jax.numpy as jnp
from jax import lax
from jax.sharding import PartitionSpec as P

step_ratio = 0.5


def passed_along(block, axis, distance):
    devices = range(lax.axis_size(axis))
    route = [(i - distance, i) for i in devices if i - distance in devices]
    return lax.ppermute(block, axis, route)


def rim_above(grid_field):
    return passed_along(grid_field, "slab", -1)


def rim_below(grid_field):
    return passed_along(grid_field, "slab", 1)


def up_diff(grid_field, along_dim):
    extent = grid_field.shape[along_dim]
    if along_dim == 1:
        shifted = jnp.concatenate([grid_field[:, 1:], rim_above(grid_field)], axis=1)
    else:
        zero_plane = jnp.zeros_like(lax.slice_in_dim(grid_field, 0, 1, axis=along_dim))
        shifted = jnp.concatenate(
            [lax.slice_in_dim(grid_field, 1, extent, axis=along_dim), zero_plane], axis=along_dim
        )
    return shifted - grid_field


def down_diff(grid_field, along_dim):
    extent = grid_field.shape[along_dim]
    if along_dim == 1:
        behind = jnp.concatenate([rim_below(grid_field), grid_field[:, :-1]], axis=1)
    else:
        zero_plane = jnp.zeros_like(lax.slice_in_dim(grid_field, 0, 1, axis=along_dim))
        behind = jnp.concatenate(
            [zero_plane, lax.slice_in_dim(grid_field, 0, extent - 1, axis=along_dim)],
            axis=along_dim,
        )
    return grid_field - behind


def shards(
    sound_speed,
    density,
    attenuation,
    wavelet,
    weights,
    emitter_group,
    emitter_cell,
    receiver_cell,
    pressure_start,
    velocity_start,
    observed,
):
    planes, width_x, width_y = sound_speed.shape
    cells_dev = planes * width_x * width_y
    group_count = lax.axis_size("grp")
    group_index = lax.axis_index("grp")
    slab_index = lax.axis_index("slab")
    shots_total = weights.shape[0]
    shots_dev = shots_total // group_count
    steps_total = observed.shape[1]
    recv_dev = observed.shape[2]
    owner_group = jnp.arange(shots_total) // shots_dev
    active = jnp.where(
        emitter_group[None, :] == owner_group[:, None], weights, jnp.zeros_like(weights)
    )
    own_active = lax.dynamic_slice_in_dim(active, group_index * shots_dev, shots_dev, 0)
    panel_piece = lax.all_gather(observed, "grp", axis=0, tiled=True)
    encoded = jnp.dot(
        own_active,
        panel_piece.reshape(panel_piece.shape[0], -1),
        preferred_element_type=jnp.float32,
    )
    local_cell = emitter_cell - slab_index * cells_dev
    inside = (local_cell >= 0) & (local_cell < cells_dev)
    safe_cell = jnp.where(inside, local_cell, 0)
    amp_terms = jnp.where(inside[None, :], own_active.astype(jnp.float32), 0.0)
    amplitude = jnp.zeros((shots_dev, cells_dev), jnp.float32).at[:, safe_cell].add(amp_terms)
    amplitude = amplitude.reshape(shots_dev, planes, width_x, width_y)
    kappa_field = density * sound_speed * sound_speed
    buoyancy = 1.0 / density
    keep_rate = 1.0 - attenuation
    pressure = pressure_start
    velocity = [velocity_start[0], velocity_start[1], velocity_start[2]]
    stored_pressure = []
    stored_div = []
    recorded = []
    for step_index in range(steps_total):
        stored_pressure.append(pressure)
        velocity = [
            velocity[dim_index] - step_ratio * buoyancy * up_diff(pressure, dim_index + 1)
            for dim_index in range(3)
        ]
        div_field = (
            down_diff(velocity[0], 1) + down_diff(velocity[1], 2) + down_diff(velocity[2], 3)
        )
        stored_div.append(div_field)
        pressure = (
            keep_rate * pressure
            - step_ratio * kappa_field * div_field
            + wavelet[step_index] * amplitude
        )
        recorded.append(pressure.reshape(shots_dev, cells_dev)[:, receiver_cell])
    residual = (
        jnp.stack(recorded, axis=1) - encoded.reshape(shots_dev, steps_total, recv_dev)
    ) / shots_total
    lam_pressure = jnp.zeros_like(pressure)
    lam_velocity = [jnp.zeros_like(pressure), jnp.zeros_like(pressure), jnp.zeros_like(pressure)]
    grad_kappa = jnp.zeros_like(pressure)
    grad_decay = jnp.zeros_like(pressure)
    for step_index in reversed(range(steps_total)):
        injected = (
            jnp.zeros((shots_dev, cells_dev), jnp.float32)
            .at[:, receiver_cell]
            .add(residual[:, step_index])
        )
        adj_field = lam_pressure + injected.reshape(pressure.shape)
        grad_decay = grad_decay - adj_field * stored_pressure[step_index]
        grad_kappa = grad_kappa - step_ratio * adj_field * stored_div[step_index]
        if step_index > 0:
            scaled = kappa_field * adj_field
            lam_velocity = [
                lam_velocity[dim_index] + step_ratio * up_diff(scaled, dim_index + 1)
                for dim_index in range(3)
            ]
            weighted = [buoyancy * lam_velocity[dim_index] for dim_index in range(3)]
            lam_pressure = keep_rate * adj_field + step_ratio * (
                down_diff(weighted[0], 1) + down_diff(weighted[1], 2) + down_diff(weighted[2], 3)
            )
    speed_term = jnp.sum(grad_kappa, axis=0) * (2.0 * density * sound_speed)
    decay_term = jnp.sum(grad_decay, axis=0)
    grad_speed, grad_atten = (
        lax.psum_scatter(speed_term, "grp", scatter_dimension=1, tiled=True),
        lax.psum_scatter(decay_term, "grp", scatter_dimension=1, tiled=True),
    )
    return (grad_speed, grad_atten)


def solution(mesh):
    return jax.shard_map(
        shards,
        mesh=mesh,
        in_specs=(
            P("slab", None, None),
            P("slab", None, None),
            P("slab", None, None),
            P(),
            P(),
            P(),
            P(),
            P("slab"),
            P("grp", "slab", None, None),
            P(None, "grp", "slab", None, None),
            P("grp", None, "slab"),
        ),
        out_specs=(P("slab", "grp", None), P("slab", "grp", None)),
        check_vma=False,
    )
```

profile of v0, /device:TPU:6, one launch (start us, length us, event | category | flops | bytes accessed | tf_op | source)
XLA Modules:
  0.0 364.0 jit_solution(9447701609415373525)
XLA Ops:
  11.0 7.6 %scatter_custom_fusion = f32[65536]{0:T(1024)S(1)} fusion(s32[1024]{0:T(1024)S(1)} %compare_select_fusion.1, f32[1024]{0:T(1024)S(1)} %bitcast.196, f32[]{:T(128)} %constant.12.clone.1), kind=kCustom, calls=%fused_computation.98 | custom fusion | flops 1024 | bytes 262148 | tf_op jit(solution)/shard_map/scatter-add | solution.py:85
  19.5 3.1 collective-permute-start.1
  22.5 3.4 broadcast_multiply_fusion.2
  29.3 2.6 collective-permute-done.2
  32.1 6.7 %collective-permute-start.3 = (f32[1,1,256,256]{3,2,1,0:T(8,128)S(1)}, f32[1,1,256,256]{3,2,1,0:T(8,128)S(1)}, u32[]{:S(2)}, u32[]{:S(2)}) collective-permute-start(f32[1,1,256,256]{3,2,1,0:T(8,128)S(1)} %get-tuple-element.42), channel_id=1, source_target_pairs={{0,8},{8,16},{16,24},{24,32},{32,40},{40,48},{48,56},{56,64},{64,7... | collective-permute-start | bytes 786440 | tf_op jit(solution)/shard_map/ppermute | solution.py:12
  42.3 3.6 collective-permute-done.4
  46.1 10.0 %collective-permute-start.5 = (f32[1,1,256,256]{3,2,1,0:T(8,128)S(1)}, f32[1,1,256,256]{3,2,1,0:T(8,128)S(1)}, u32[]{:S(2)}, u32[]{:S(2)}) collective-permute-start(f32[1,1,256,256]{3,2,1,0:T(8,128)S(1)} %get-tuple-element.39), channel_id=1, source_target_pairs={{0,8},{8,16},{16,24},{24,32},{32,40},{40,48},{48,56},{56,64},{64,7... | collective-permute-start | bytes 786440 | tf_op jit(solution)/shard_map/ppermute | solution.py:12
  58.1 1.4 collective-permute-start.6
  59.7 3.6 collective-permute-done.6
  64.1 12.0 %collective-permute-start.7 = (f32[1,1,256,256]{3,2,1,0:T(8,128)}, f32[1,1,256,256]{3,2,1,0:T(8,128)S(1)}, u32[]{:S(2)}, u32[]{:S(2)}) collective-permute-start(f32[1,1,256,256]{3,2,1,0:T(8,128)} %get-tuple-element.36), channel_id=1, source_target_pairs={{0,8},{8,16},{16,24},{24,32},{32,40},{40,48},{48,56},{56,64},{64,7... | collective-permute-start | bytes 786440 | tf_op jit(solution)/shard_map/ppermute | solution.py:12
  80.2 30.4 %all-gather.2.cloned.1.call-done = bf16[1024,4,128]{2,1,0:T(4,128)(2,1)} async-done(((bf16[128,4,128]{2,1,0:T(4,128)(2,1)}), bf16[1024,4,128]{2,1,0:T(4,128)(2,1)}) %all-gather.2.cloned.1.call-update) | async-done | bytes 1048592 | tf_op jit(solution)/shard_map/all_gather | solution.py:75
  110.6 1.5 fusion
  112.1 1.8 fusion.21
  115.2 1.3 scatter_custom_fusion.1
  118.2 1.9 collective-permute-done.8
  120.9 9.1 %collective-permute-start.9 = (f32[1,1,256,256]{3,2,1,0:T(8,128)}, f32[1,1,256,256]{3,2,1,0:T(8,128)}, u32[]{:S(2)}, u32[]{:S(2)}) collective-permute-start(f32[1,1,256,256]{3,2,1,0:T(8,128)} %get-tuple-element.33), channel_id=1, source_target_pairs={{0,8},{8,16},{16,24},{24,32},{32,40},{40,48},{48,56},{56,64},{64,7... | collective-permute-start | bytes 786440 | tf_op jit(solution)/shard_map/ppermute | solution.py:12
  134.1 2.9 collective-permute-done.10
  138.2 8.1 %collective-permute-start.11 = (f32[1,1,256,256]{3,2,1,0:T(8,128)}, f32[1,1,256,256]{3,2,1,0:T(8,128)}, u32[]{:S(2)}, u32[]{:S(2)}) collective-permute-start(f32[1,1,256,256]{3,2,1,0:T(8,128)} %get-tuple-element.6), channel_id=1, source_target_pairs={{0,8},{8,16},{16,24},{24,32},{32,40},{40,48},{48,56},{56,64},{64,7... | collective-permute-start | bytes 786440 | tf_op jit(solution)/shard_map/ppermute | solution.py:12
  146.3 1.3 scatter_custom_fusion.3
  151.2 2.2 collective-permute-done.12
  154.3 8.1 %collective-permute-start.13 = (f32[1,1,256,256]{3,2,1,0:T(8,128)}, f32[1,1,256,256]{3,2,1,0:T(8,128)}, u32[]{:S(2)}, u32[]{:S(2)}) collective-permute-start(f32[1,1,256,256]{3,2,1,0:T(8,128)} %get-tuple-element.30), channel_id=1, source_target_pairs={{0,8},{8,16},{16,24},{24,32},{32,40},{40,48},{48,56},{56,64},{64,7... | collective-permute-start | bytes 786440 | tf_op jit(solution)/shard_map/ppermute | solution.py:12
  163.9 2.1 subtract_bitcast_fusion
  167.7 99.3 %reduce-scatter.3.cloned.1.call-done = f32[1,32,256]{2,1,0:T(8,128)} async-done(((f32[1,256,256]{2,1,0:T(8,128)}), f32[1,32,256]{2,1,0:T(8,128)}) %reduce-scatter.3.cloned.1.call-update) | async-done | bytes 32784 | tf_op jit(solution)/shard_map/reduce_scatter | solution.py:140
  267.0 90.5 %reduce-scatter.5.cloned.1.call-done = f32[1,32,256]{2,1,0:T(8,128)} async-done(((f32[1,256,256]{2,1,0:T(8,128)}), f32[1,32,256]{2,1,0:T(8,128)}) %reduce-scatter.5.cloned.1.call-update) | async-done | bytes 32784 | tf_op jit(solution)/shard_map/reduce_scatter | solution.py:141
  (126 shorter events, 34.8 us)
Async XLA Ops:
  7.2 103.4 %all-gather.2.cloned.1.call-start = ((), (), s32[]{:S(2)}) async-start(), calls=%async_computation.2 | async-start | bytes 1179648 | tf_op jit(solution)/shard_map/all_gather | solution.py:75
  7.2 12.1 %collective-permute-start = (f32[1,1,256,256]{3,2,1,0:T(8,128)}, f32[1,1,256,256]{3,2,1,0:T(8,128)S(1)}, u32[]{:S(2)}, u32[]{:S(2)}) collective-permute-start(f32[1,1,256,256]{3,2,1,0:T(8,128)} %param.19), channel_id=1, source_target_pairs={{8,0},{16,8},{24,16},{32,24},{40,32},{48,40},{56,48},{64,56},{72,6... | collective-permute-start | bytes 786440 | tf_op jit(solution)/shard_map/ppermute | solution.py:12
  9.2 10.1 %copy-start.20 = (f32[3,1,1,256,256]{4,3,2,1,0:T(8,128)S(1)}, f32[3,1,1,256,256]{4,3,2,1,0:T(8,128)}, u32[]{:S(2)}) copy-start(f32[3,1,1,256,256]{4,3,2,1,0:T(8,128)} %param.20) | copy-start | bytes 2359300
  10.5 8.8 %copy-start = (f32[1,256,256]{2,1,0:T(8,128)S(1)}, f32[1,256,256]{2,1,0:T(8,128)}, u32[]{:S(2)}) copy-start(f32[1,256,256]{2,1,0:T(8,128)} %param.12) | copy-start | bytes 786436
  11.0 7.6 %copy-start.22 = (f32[4]{0:T(128)S(1)}, f32[4]{0:T(128)}, u32[]{:S(2)}) copy-start(f32[4]{0:T(128)} %param.14) | copy-start | bytes 52
  19.5 6.6 %collective-permute-start.1 = (f32[1,1,256,256]{3,2,1,0:T(8,128)S(1)}, f32[1,1,256,256]{3,2,1,0:T(8,128)S(1)}, u32[]{:S(2)}, u32[]{:S(2)}) collective-permute-start(f32[1,1,256,256]{3,2,1,0:T(8,128)S(1)} %get-tuple-element.23), channel_id=1, source_target_pairs={{0,8},{8,16},{16,24},{24,32},{32,40},{40,48},{48,56},{56,64},{64,7... | collective-permute-start | bytes 786440 | tf_op jit(solution)/shard_map/ppermute | solution.py:12
  27.9 4.1 %collective-permute-start.2 = (f32[1,1,256,256]{3,2,1,0:T(8,128)S(1)}, f32[1,1,256,256]{3,2,1,0:T(8,128)S(1)}, u32[]{:S(2)}, u32[]{:S(2)}) collective-permute-start(f32[1,1,256,256]{3,2,1,0:T(8,128)S(1)} %get-tuple-element.20), channel_id=1, source_target_pairs={{8,0},{16,8},{24,16},{32,24},{40,32},{48,40},{56,48},{64,56},{72,6... | collective-permute-start | bytes 786440 | tf_op jit(solution)/shard_map/ppermute | solution.py:12
  32.1 7.8 %collective-permute-start.3 = (f32[1,1,256,256]{3,2,1,0:T(8,128)S(1)}, f32[1,1,256,256]{3,2,1,0:T(8,128)S(1)}, u32[]{:S(2)}, u32[]{:S(2)}) collective-permute-start(f32[1,1,256,256]{3,2,1,0:T(8,128)S(1)} %get-tuple-element.42), channel_id=1, source_target_pairs={{0,8},{8,16},{16,24},{24,32},{32,40},{40,48},{48,56},{56,64},{64,7... | collective-permute-start | bytes 786440 | tf_op jit(solution)/shard_map/ppermute | solution.py:12
  38.8 228.2 %reduce-scatter.3.cloned.1.call-start = ((), (), s32[]{:S(2)}) async-start(), calls=%async_computation.3 | async-start | bytes 294912 | tf_op jit(solution)/shard_map/reduce_scatter | solution.py:140
  40.8 5.1 %collective-permute-start.4 = (f32[1,1,256,256]{3,2,1,0:T(8,128)S(1)}, f32[1,1,256,256]{3,2,1,0:T(8,128)S(1)}, u32[]{:S(2)}, u32[]{:S(2)}) collective-permute-start(f32[1,1,256,256]{3,2,1,0:T(8,128)S(1)} %get-tuple-element.18), channel_id=1, source_target_pairs={{8,0},{16,8},{24,16},{32,24},{40,32},{48,40},{56,48},{64,56},{72,6... | collective-permute-start | bytes 786440 | tf_op jit(solution)/shard_map/ppermute | solution.py:12
  42.3 13.8 %copy-start.11 = (f32[65536]{0:T(1024)S(1)}, f32[65536]{0:T(1024)}, u32[]{:S(2)}) copy-start(f32[65536]{0:T(1024)} %get-tuple-element.46) | copy-start | bytes 786436
  46.1 11.1 %collective-permute-start.5 = (f32[1,1,256,256]{3,2,1,0:T(8,128)S(1)}, f32[1,1,256,256]{3,2,1,0:T(8,128)S(1)}, u32[]{:S(2)}, u32[]{:S(2)}) collective-permute-start(f32[1,1,256,256]{3,2,1,0:T(8,128)S(1)} %get-tuple-element.39), channel_id=1, source_target_pairs={{0,8},{8,16},{16,24},{24,32},{32,40},{40,48},{48,56},{56,64},{64,7... | collective-permute-start | bytes 786440 | tf_op jit(solution)/shard_map/ppermute | solution.py:12
  58.1 5.2 %collective-permute-start.6 = (f32[1,1,256,256]{3,2,1,0:T(8,128)S(1)}, f32[1,1,256,256]{3,2,1,0:T(8,128)S(1)}, u32[]{:S(2)}, u32[]{:S(2)}) collective-permute-start(f32[1,1,256,256]{3,2,1,0:T(8,128)S(1)} %get-tuple-element.16), channel_id=1, source_target_pairs={{8,0},{16,8},{24,16},{32,24},{40,32},{48,40},{56,48},{64,56},{72,6... | collective-permute-start | bytes 786440 | tf_op jit(solution)/shard_map/ppermute | solution.py:12
  59.7 16.5 %copy-start.10 = (f32[65536]{0:T(1024)S(1)}, f32[65536]{0:T(1024)}, u32[]{:S(2)}) copy-start(f32[65536]{0:T(1024)} %get-tuple-element.48) | copy-start | bytes 786436
  64.1 47.9 %collective-permute-start.7 = (f32[1,1,256,256]{3,2,1,0:T(8,128)}, f32[1,1,256,256]{3,2,1,0:T(8,128)S(1)}, u32[]{:S(2)}, u32[]{:S(2)}) collective-permute-start(f32[1,1,256,256]{3,2,1,0:T(8,128)} %get-tuple-element.36), channel_id=1, source_target_pairs={{0,8},{8,16},{16,24},{24,32},{32,40},{40,48},{48,56},{56,64},{64,7... | collective-permute-start | bytes 786440 | tf_op jit(solution)/shard_map/ppermute | solution.py:12
  116.7 3.4 collective-permute-start.8
  120.9 10.5 %collective-permute-start.9 = (f32[1,1,256,256]{3,2,1,0:T(8,128)}, f32[1,1,256,256]{3,2,1,0:T(8,128)}, u32[]{:S(2)}, u32[]{:S(2)}) collective-permute-start(f32[1,1,256,256]{3,2,1,0:T(8,128)} %get-tuple-element.33), channel_id=1, source_target_pairs={{0,8},{8,16},{16,24},{24,32},{32,40},{40,48},{48,56},{56,64},{64,7... | collective-permute-start | bytes 786440 | tf_op jit(solution)/shard_map/ppermute | solution.py:12
  132.7 4.4 %collective-permute-start.10 = (f32[1,1,256,256]{3,2,1,0:T(8,128)S(1)}, f32[1,1,256,256]{3,2,1,0:T(8,128)S(1)}, u32[]{:S(2)}, u32[]{:S(2)}) collective-permute-start(f32[1,1,256,256]{3,2,1,0:T(8,128)S(1)} %get-tuple-element.12), channel_id=1, source_target_pairs={{8,0},{16,8},{24,16},{32,24},{40,32},{48,40},{56,48},{64,56},{72,6... | collective-permute-start | bytes 786440 | tf_op jit(solution)/shard_map/ppermute | solution.py:12
  134.0 3.1 copy-start.16
  134.0 3.1 copy-start.4
  138.2 10.2 %collective-permute-start.11 = (f32[1,1,256,256]{3,2,1,0:T(8,128)}, f32[1,1,256,256]{3,2,1,0:T(8,128)}, u32[]{:S(2)}, u32[]{:S(2)}) collective-permute-start(f32[1,1,256,256]{3,2,1,0:T(8,128)} %get-tuple-element.6), channel_id=1, source_target_pairs={{0,8},{8,16},{16,24},{24,32},{32,40},{40,48},{48,56},{56,64},{64,7... | collective-permute-start | bytes 786440 | tf_op jit(solution)/shard_map/ppermute | solution.py:12
  149.7 3.7 %collective-permute-start.12 = (f32[1,1,256,256]{3,2,1,0:T(8,128)S(1)}, f32[1,1,256,256]{3,2,1,0:T(8,128)S(1)}, u32[]{:S(2)}, u32[]{:S(2)}) collective-permute-start(f32[1,1,256,256]{3,2,1,0:T(8,128)S(1)} %get-tuple-element.4), channel_id=1, source_target_pairs={{8,0},{16,8},{24,16},{32,24},{40,32},{48,40},{56,48},{64,56},{72,6... | collective-permute-start | bytes 786440 | tf_op jit(solution)/shard_map/ppermute | solution.py:12
  154.3 9.5 %collective-permute-start.13 = (f32[1,1,256,256]{3,2,1,0:T(8,128)}, f32[1,1,256,256]{3,2,1,0:T(8,128)}, u32[]{:S(2)}, u32[]{:S(2)}) collective-permute-start(f32[1,1,256,256]{3,2,1,0:T(8,128)} %get-tuple-element.30), channel_id=1, source_target_pairs={{0,8},{8,16},{16,24},{24,32},{32,40},{40,48},{48,56},{56,64},{64,7... | collective-permute-start | bytes 786440 | tf_op jit(solution)/shard_map/ppermute | solution.py:12
  167.0 190.5 %reduce-scatter.5.cloned.1.call-start = ((), (), s32[]{:S(2)}) async-start(), calls=%async_computation.4 | async-start | bytes 294912 | tf_op jit(solution)/shard_map/reduce_scatter | solution.py:141
  (19 other events, 33.8 us)
Sparse Core Ops, SparseCore 0:
  38.9 71.6 all-gather.1
  167.1 99.8 reduce-scatter.2
  272.6 84.7 reduce-scatter.4
where the time goes:
time: 365 us; the launch traced here: 364 us
  waiting for transfers between devices  240 us (66%)
  starting transfers between devices  66.3 us (18%)
  other arithmetic  30.4 us (8%)
  between operations  14.5 us (4%)
  local copies, waits for them, and re-layouts  11.4 us (3%)
    reduce_scatter x1, waiting for transfers between devices, shards(): lax.psum_scatter(speed_term, 'grp', scatter_dimension=1, tiled=True)  99.3 us
    reduce_scatter x1, waiting for transfers between devices, shards(): lax.psum_scatter(decay_term, 'grp', scatter_dimension=1, tiled=True)  90.5 us
    ppermute x14, starting transfers between devices, passed_along(): return lax.ppermute(block, axis, route)  66.2 us
    all_gather x1, waiting for transfers between devices, shards(): panel_piece = lax.all_gather(observed, 'grp', axis=0, tiled=True)  30.4 us
    ppermute x14, waiting for transfers between devices, passed_along(): return lax.ppermute(block, axis, route)  19 us
    scatter-add x1, other arithmetic, shards(): jnp.zeros((shots_dev, cells_dev), jnp.float32).at[:, safe_cell]  7.59 us
  transfers between devices with their start and end apart: 17, of which 11 were waited for; matrix products, arithmetic and copies ran while one was open for 7% of the time, Pallas kernels for 0%

commit v1 on v0

v1 whole, which is shorter than its diff:
```python
import functools
import jax
import jax.numpy as jnp
from jax import lax
from jax.experimental import pallas as pl
from jax.experimental.pallas import tpu as pltpu
from jax.sharding import PartitionSpec as P

MESH = pl.DeviceIdType.MESH
HALF = 0.5
F32 = jnp.float32
BF16 = jnp.bfloat16


def split3(v):
    hi = v.astype(BF16)
    rest = v - hi.astype(F32)
    mid = rest.astype(BF16)
    low = (rest - mid.astype(F32)).astype(BF16)
    return hi, mid, low


def kernel(
    n_slab, n_grp,
    wav, speed_h, dens_h, atten_h, press_h, vel_h, weights, group, ecell, rcell, obs,
    out_s, out_a,
    speed, dens, atten, press, vel, wup, bup, pdn, wlow, blow,
    pabove, pbelow, sabove, sbelow, scaled, encsend, encrecv, grad, gradrecv,
    load_sem, halo_send, halo_recv, enc_send, enc_recv, grad_send, grad_recv,
):
    steps = 4
    slab = lax.axis_index("slab")
    grp = lax.axis_index("grp")
    above = lax.rem(slab + 1, n_slab)
    below = lax.rem(slab + n_slab - 1, n_slab)

    loads = [
        pltpu.make_async_copy(src, dst, load_sem.at[i])
        for i, (src, dst) in enumerate([
            (press_h.at[0, 0], press.at[0]), (dens_h.at[0], dens), (vel_h.at[:, 0, 0], vel),
            (speed_h.at[0], speed), (atten_h.at[0], atten),
        ])
    ]
    for c in loads:
        c.start()

    barrier = pltpu.get_barrier_semaphore()
    for s in (above, below):
        pl.semaphore_signal(barrier, inc=1, device_id=(s, grp), device_id_type=MESH)
    for d in range(1, n_grp):
        pl.semaphore_signal(
            barrier, inc=1, device_id=(slab, lax.rem(grp + d, n_grp)), device_id_type=MESH)
    pl.semaphore_wait(barrier, n_grp + 1)

    def send(src, dst, to, k):
        c = pltpu.make_async_remote_copy(
            src_ref=src, dst_ref=dst, send_sem=halo_send.at[k], recv_sem=halo_recv.at[k],
            device_id=(to, grp), device_id_type=MESH)
        c.start()
        return c

    pending = []
    for c in loads[:3]:
        c.wait()
    p0_down = send(press.at[0], pdn, below, 0)
    buoy = 1.0 / dens[...]
    bup[...] = buoy
    wup[...] = vel[0] + HALF * buoy * press[0]
    w_up = send(wup, wlow, above, 1)
    b_up = send(bup, blow, above, 2)

    wall = weights[...].astype(F32)
    shot_row = lax.broadcasted_iota(jnp.int32, wall.shape, 0)
    active = jnp.where(group[...] == shot_row, wall, 0.0)
    own = jnp.sum(jnp.where(shot_row == grp, active, 0.0), axis=0, keepdims=True)
    emit = wall.shape[1]
    ec = ecell[...] - slab * 65536
    inside = (ec >= 0) & (ec < 65536)
    ex = jnp.where(inside, ec >> 8, -1)
    ey = ec & 255
    row_e = lax.broadcasted_iota(jnp.int32, (256, emit), 0)
    ax = jnp.where(row_e == ex, own, 0.0).astype(BF16)
    ay = jnp.where(row_e == ey, 1.0, 0.0).astype(BF16)
    nt = (((1,), (1,)), ((), ()))
    amp = lax.dot_general(ax, ay, nt, preferred_element_type=F32)

    e_dev = obs.shape[0]
    eoff = pl.multiple_of(grp * e_dev, 128)
    wdev = weights[:, pl.ds(eoff, e_dev)].astype(F32)
    gdev = group[:, pl.ds(eoff, e_dev)]
    act_dev = jnp.where(
        gdev == lax.broadcasted_iota(jnp.int32, wdev.shape, 0), wdev, 0.0).astype(BF16)
    er = lax.broadcasted_iota(jnp.int32, (e_dev, e_dev * steps), 0)
    el = lax.broadcasted_iota(jnp.int32, (e_dev, e_dev * steps), 1)
    expand = jnp.where((el >> 2) == er, 1.0, 0.0).astype(BF16)
    wide = jnp.dot(act_dev, expand, preferred_element_type=F32).astype(BF16)
    rr = lax.broadcasted_iota(jnp.int32, (8 * n_grp, n_grp), 0)
    rl = lax.broadcasted_iota(jnp.int32, (8 * n_grp, n_grp), 1)
    rows = jnp.where((rr >> 3) == rl, 1.0, 0.0).astype(BF16)
    tall = jnp.dot(rows, wide, preferred_element_type=F32)
    tr = lax.broadcasted_iota(jnp.int32, tall.shape, 0)
    tl = lax.broadcasted_iota(jnp.int32, tall.shape, 1)
    lhs = jnp.where((tr & 7) == (tl & 3), tall, 0.0).astype(BF16)
    flat = obs[...].astype(F32).reshape(e_dev * steps, obs.shape[2]).astype(BF16)
    part = jnp.dot(lhs, flat, preferred_element_type=F32)
    encsend[...] = part.reshape(encsend.shape)
    for d in range(1, n_grp):
        peer = lax.rem(grp + d, n_grp)
        c = pltpu.make_async_remote_copy(
            src_ref=encsend.at[peer], dst_ref=encrecv.at[d], send_sem=enc_send.at[d],
            recv_sem=enc_recv.at[d], device_id=(slab, peer), device_id_type=MESH)
        c.start()
        pending.append(c)
    enc_copies = list(pending)

    rc = rcell[...]
    row_r = lax.broadcasted_iota(jnp.int32, (256, rc.shape[1]), 0)
    rx = jnp.where(row_r == (rc >> 8), 1.0, 0.0)
    ry = jnp.where(row_r == (rc & 255), 1.0, 0.0).astype(BF16)
    ry3 = jnp.concatenate([ry, ry, ry], axis=1)

    def record(field):
        total = 0.0
        for piece in split3(field):
            total = total + jnp.dot(piece, ry, preferred_element_type=F32)
        return jnp.sum(total * rx, axis=0, keepdims=True)

    def inject(values):
        pieces = [(rx * v.astype(F32)).astype(BF16) for v in split3(values)]
        return lax.dot_general(
            jnp.concatenate(pieces, axis=1), ry3, nt, preferred_element_type=F32)

    xi = lax.broadcasted_iota(jnp.int32, (256, 256), 0)
    yi = lax.broadcasted_iota(jnp.int32, (256, 256), 1)

    def up_x(f):
        return jnp.where(xi == 255, 0.0, pltpu.roll(f, 255, 0)) - f

    def up_y(f):
        return jnp.where(yi == 255, 0.0, pltpu.roll(f, 255, 1)) - f

    def down_x(f):
        return f - jnp.where(xi == 0, 0.0, pltpu.roll(f, 1, 0))

    def down_y(f):
        return f - jnp.where(yi == 0, 0.0, pltpu.roll(f, 1, 1))

    has_above = slab < n_slab - 1
    has_below = slab > 0
    for c in loads[3:]:
        c.wait()
    kappa = dens[...] * speed[...] * speed[...]
    keep = 1.0 - atten[...]

    divs = []
    recorded = []
    pz, px, py = vel[0], vel[1], vel[2]
    p = press[0]
    p0_down.wait_recv()
    w_up.wait_recv()
    b_up.wait_recv()
    b_low = jnp.where(has_below, blow[...], 0.0)
    for t in range(steps):
        if t == 0:
            pa = jnp.where(has_above, pdn[...], 0.0)
            pzl = jnp.where(has_below, wlow[...], 0.0) - HALF * b_low * p
        else:
            dn = send(press.at[t], pabove.at[t - 1], below, 3 + 2 * (t - 1))
            up = send(press.at[t], pbelow.at[t - 1], above, 4 + 2 * (t - 1))
            dn.wait_recv()
            up.wait_recv()
            pending += [dn, up]
            pa = jnp.where(has_above, pabove[t - 1], 0.0)
            pzl = pzl - HALF * b_low * (p - pbelow[t - 1])
        pz = pz - HALF * buoy * (pa - p)
        px = px - HALF * buoy * up_x(p)
        py = py - HALF * buoy * up_y(p)
        div = pz - pzl + down_x(px) + down_y(py)
        divs.append(div)
        p = keep * p - HALF * kappa * div + wav[t] * amp
        if t < steps - 1:
            press[t + 1] = p
        recorded.append(record(p))

    for c in enc_copies:
        c.wait_recv()
    enc = encsend[grp]
    for d in range(1, n_grp):
        enc = enc + encrecv[d]

    lp = jnp.zeros((256, 256), F32)
    lz = lx = ly = lzl = lp
    gk = gd = lp
    for t in reversed(range(steps)):
        residual = (recorded[t] - enc[t:t + 1]) * (1.0 / n_grp)
        adj = lp + inject(residual)
        gd = gd - adj * press[t]
        gk = gk - HALF * adj * divs[t]
        if t > 0:
            s = kappa * adj
            scaled[t - 1] = s
            dn = send(scaled.at[t - 1], sabove.at[t - 1], below, 9 + 2 * (t - 1))
            up = send(scaled.at[t - 1], sbelow.at[t - 1], above, 10 + 2 * (t - 1))
            pending += [dn, up]
            dn.wait_recv()
            up.wait_recv()
            sa = jnp.where(has_above, sabove[t - 1], 0.0)
            lz = lz + HALF * (sa - s)
            lzl = lzl + HALF * (s - sbelow[t - 1])
            lx = lx + HALF * up_x(s)
            ly = ly + HALF * up_y(s)
            lp = keep * adj + HALF * (
                buoy * lz - b_low * lzl + down_x(buoy * lx) + down_y(buoy * ly))
    grad[0] = gk * (2.0 * dens[...] * speed[...])
    grad[1] = gd
    rows_out = 256 // n_grp
    copies = []
    for d in range(1, n_grp):
        peer = lax.rem(grp + d, n_grp)
        c = pltpu.make_async_remote_copy(
            src_ref=grad.at[:, pl.ds(pl.multiple_of(peer * rows_out, rows_out), rows_out)],
            dst_ref=gradrecv.at[d], send_sem=grad_send.at[d],
            recv_sem=grad_recv.at[d], device_id=(slab, peer), device_id_type=MESH)
        c.start()
        copies.append(c)
    total = grad[:, pl.ds(pl.multiple_of(grp * rows_out, rows_out), rows_out)]
    for d in range(1, n_grp):
        copies[d - 1].wait_recv()
        total = total + gradrecv[d]
    out_s[0] = total[0]
    out_a[0] = total[1]
    for c in [p0_down, w_up, b_up] + pending + copies:
        c.wait_send()


def shards(
    n_slab, n_grp,
    sound_speed, density, attenuation, wavelet, weights, emitter_group, emitter_cell,
    receiver_cell, pressure_start, velocity_start, observed,
):
    vmem = pl.BlockSpec(memory_space=pltpu.VMEM)
    hbm = pl.BlockSpec(memory_space=pl.ANY)
    smem = pl.BlockSpec(memory_space=pltpu.SMEM)
    rows = 256 // n_grp
    plane = lambda *n: pltpu.VMEM(n + (256, 256), F32)
    out = jax.ShapeDtypeStruct((1, rows, 256), F32)
    dma = pltpu.SemaphoreType.DMA
    return pl.pallas_call(
        functools.partial(kernel, n_slab, n_grp),
        out_shape=(out, out),
        in_specs=[smem] + [hbm] * 5 + [vmem] * 5,
        out_specs=(vmem, vmem),
        scratch_shapes=[
            plane(), plane(), plane(), plane(4), plane(3), plane(), plane(), plane(), plane(),
            plane(), plane(3), plane(3), plane(3), plane(3), plane(3),
            pltpu.VMEM((n_grp, 8, 128), F32), pltpu.VMEM((n_grp, 8, 128), F32),
            plane(2), pltpu.VMEM((n_grp, 2, rows, 256), F32),
            dma((5,)), dma((15,)), dma((15,)), dma((n_grp,)), dma((n_grp,)),
            dma((n_grp,)), dma((n_grp,)),
        ],
        compiler_params=pltpu.CompilerParams(
            collective_id=0, has_side_effects=True, vmem_limit_bytes=48 * 1024 * 1024),
    )(
        wavelet, sound_speed, density, attenuation, pressure_start, velocity_start, weights,
        emitter_group.reshape(1, -1), emitter_cell.reshape(1, -1),
        receiver_cell.reshape(1, -1), observed,
    )


def solution(mesh):
    return jax.shard_map(
        functools.partial(shards, mesh.shape["slab"], mesh.shape["grp"]),
        mesh=mesh,
        in_specs=(
            P("slab", None, None),
            P("slab", None, None),
            P("slab", None, None),
            P(),
            P(),
            P(),
            P(),
            P("slab"),
            P("grp", "slab", None, None),
            P(None, "grp", "slab", None, None),
            P("grp", None, "slab"),
        ),
        out_specs=(P("slab", "grp", None), P("slab", "grp", None)),
        check_vma=False,
    )
```

time: 365 us -> 104 us (0.28)
  waiting for transfers between devices: 240 us -> 0 us
  Pallas kernels: 0 us -> 93.3 us
  starting transfers between devices: 66.3 us -> 0 us
  other arithmetic: 30.4 us -> 0 us
  between operations: 14.5 us -> 0.68 us
    reduce_scatter x2 -> x0, waiting for transfers between devices: 190 us -> none  [the longest x1 99.3 us: shards(): lax.psum_scatter(speed_term, 'grp', scatter_dimension=1, tiled=True)]
    pallas_call x0 -> x1, Pallas kernels: none -> 93.3 us  [shards(): pl.pallas_call(functools.partial(kernel, n_slab, n_grp), out_shape=(out,...]
    ppermute x14 -> x0, starting transfers between devices: 66.2 us -> none  [passed_along(): return lax.ppermute(block, axis, route)]
    all_gather x1 -> x0, waiting for transfers between devices: 30.4 us -> none  [shards(): panel_piece = lax.all_gather(observed, 'grp', axis=0, tiled=True)]
    ppermute x14 -> x0, waiting for transfers between devices: 19 us -> none  [passed_along(): return lax.ppermute(block, axis, route)]
    scatter-add x5 -> x0, other arithmetic: 12.9 us -> none  [the longest x1 7.59 us: shards(): jnp.zeros((shots_dev, cells_dev), jnp.float32).at[:, safe_cell]]
    mul x8 -> x0, other arithmetic: 9.56 us -> none  [the longest x1 3.38 us: shards(): wavelet[step_index] * amplitude]
    unnamed x56 -> x24, local copies, waits for them, and re-layouts: 2.79 us -> 9.14 us
  transfers between devices with their start and end apart: 17 -> 0, of which waited for: 11 -> 0; matrix products, arithmetic and copies ran while one was open for 7% -> 0% of each run, Pallas kernels for 0% -> 0%
where the time goes in v1:
time: 104 us; the launch traced here: 103 us
  Pallas kernels  93.3 us (90%)
  local copies, waits for them, and re-layouts  9.14 us (9%)
    pallas_call x1, Pallas kernels, shards(): pl.pallas_call(functools.partial(kernel, n_slab, n_grp), out_shape=(out,...  93.3 us
    unnamed x24, local copies, waits for them, and re-layouts  9.14 us

profile of v1, /device:TPU:6, one launch (start us, length us, event | category | flops | bytes accessed | tf_op | source)
XLA Modules:
  0.0 103.1 jit_solution(15408402310326534282)
XLA Ops:
  0.6 0.0 copy-start.7
  0.6 0.0 copy-start.9
  0.7 0.0 copy-start.10
  0.7 0.7 copy-done.7
  1.3 0.0 copy-done.9
  1.3 0.0 copy-done.10
  1.3 0.0 copy-start
  1.3 1.1 %copy-done = f32[3,1,1,256,256]{4,3,2,1,0:T(8,128)S(1)} copy-done((f32[3,1,1,256,256]{4,3,2,1,0:T(8,128)S(1)}, f32[3,1,1,256,256]{4,3,2,1,0:T(8,128)}, u32[]{:S(2)}) %copy-start) | copy-done | bytes 786456
  2.5 0.0 copy-start.1
  2.5 0.9 copy-done.1
  3.4 0.0 copy-start.2
  3.4 0.9 copy-done.2
  4.4 0.0 copy-start.3
  4.4 0.9 copy-done.3
  5.3 0.0 copy-start.4
  5.3 0.9 copy-done.4
  6.3 0.0 copy-start.5
  6.3 0.9 copy-done.5
  7.2 0.7 copy-done.6
  7.9 0.0 copy-start.8
  7.9 0.7 copy-done.8
  8.6 93.3 %shard_map.122 = (f32[1,32,256]{2,1,0:T(8,128)S(1)}, f32[1,32,256]{2,1,0:T(8,128)S(1)}) custom-call(f32[4]{0:T(128)S(1)} %copy-done.9, f32[1,256,256]{2,1,0:T(8,128)S(1)} %copy-done.1, f32[1,256,256]{2,1,0:T(8,128)S(1)} %copy-done.2, f32[1,256,256]{2,1,0:T(8,128)S(1)} %copy-done.3, f32[1,1,256,256]{3,2,1,0:T(8,128)S(1)} %copy-done.4, ...), custom_call_target="tpu_custom_call" | custom-call | tf_op jit(solution)/shard_map/pallas_call | solution.py:248
  101.9 0.6 copy.15
  102.5 0.6 copy.16
  (1 shorter events, 0.0 us)
Async XLA Ops:
  0.6 0.7 copy-start.7
  0.6 0.7 copy-start.9
  0.7 0.7 copy-start.10
  1.3 1.1 %copy-start = (f32[3,1,1,256,256]{4,3,2,1,0:T(8,128)S(1)}, f32[3,1,1,256,256]{4,3,2,1,0:T(8,128)}, u32[]{:S(2)}) copy-start(f32[3,1,1,256,256]{4,3,2,1,0:T(8,128)} %vel_h.1) | copy-start | bytes 2359300
  2.5 0.9 copy-start.1
  3.4 0.9 copy-start.2
  4.4 0.9 copy-start.3
  5.3 0.9 copy-start.4
  6.3 0.9 copy-start.5
  7.2 0.7 copy-start.6
  7.9 0.7 copy-start.8

commit v2 on v1

v2 whole, which is shorter than its diff:
```python
import functools
import jax
import jax.numpy as jnp
from jax import lax
from jax.experimental import pallas as pl
from jax.experimental.pallas import tpu as pltpu
from jax.sharding import PartitionSpec as P

MESH = pl.DeviceIdType.MESH
HALF = 0.5
F32 = jnp.float32
BF16 = jnp.bfloat16


I16 = jnp.int16
I32 = jnp.int32
TOP = 32767.0
NT_DOT = (((1,), (1,)), ((), ()))


def split2(v):
    hi = v.astype(BF16)
    return hi, (v - hi.astype(F32)).astype(BF16)


def split3(v):
    hi = v.astype(BF16)
    rest = v - hi.astype(F32)
    mid = rest.astype(BF16)
    return hi, mid, (rest - mid.astype(F32)).astype(BF16)


def code(v):
    return jnp.round(v).astype(I32).astype(I16)


def decode(v):
    return v.astype(I32).astype(F32)


def code_root(v, top):
    root = jnp.sqrt(jnp.abs(v) * (1.0 / top)) * TOP
    return code(jnp.where(v < 0.0, -root, root))


def decode_root(v):
    u = decode(v)
    return u * jnp.abs(u)


def top_of(v):
    return jnp.max(jnp.max(jnp.abs(v), axis=0, keepdims=True), axis=1, keepdims=True)


P_MAX = 6.0
W_MAX = 7.3
B_MID = 1.0714286
B_MAX = 0.3573


def kernel(
    n_slab, n_grp,
    wav, speed_h, dens_h, atten_h, press_h, vel_h, weights_h, group_h, ecell_h, rcell_h, obs_h,
    out_s, out_a,
    speed, dens, atten, press, vel, weights, group, ecell, obs, rcs,
    p0_out, w_out, b_out, p1_out, s1_out, p0_in, w_in, b_in, p1_in, s1_in,
    p1_scale, p1_scale_in, p2_out, p2_in, far_out, far_in, part_out, part_in, fix_out, fix_in,
    res_out, res_in, s1_scale, s1_scale_in,
    encsend, encrecv, grad, coded, gradrecv, gscale, gscale_in,
    load_sem, halo_send, halo_recv, enc_send, enc_recv, grad_send, grad_recv, gs_send, gs_recv,
):
    steps = 4
    slab = lax.axis_index("slab")
    grp = lax.axis_index("grp")
    above = lax.rem(slab + 1, n_slab)
    below = lax.rem(slab + n_slab - 1, n_slab)

    loads = [
        pltpu.make_async_copy(src, dst, load_sem.at[i])
        for i, (src, dst) in enumerate([
            (press_h.at[0, 0], press.at[0]), (dens_h.at[0], dens), (vel_h.at[:, 0, 0], vel),
            (rcell_h, rcs.at[2]), (weights_h, weights), (group_h, group), (obs_h, obs),
            (ecell_h, ecell), (speed_h.at[0], speed), (atten_h.at[0], atten),
        ])
    ]
    for c in loads:
        c.start()

    near = {d: lax.rem(slab + n_slab + d, n_slab) for d in (-2, -1, 1, 2)}
    barrier = pltpu.get_barrier_semaphore()
    for s in near.values():
        pl.semaphore_signal(barrier, inc=1, device_id=(s, grp), device_id_type=MESH)
    for d in range(1, n_grp):
        pl.semaphore_signal(
            barrier, inc=1, device_id=(slab, lax.rem(grp + d, n_grp)), device_id_type=MESH)

    for c in loads[:3]:
        c.wait()
    p0_out[...] = code(press[0] * (TOP / P_MAX))
    buoy = 1.0 / dens[...]
    w_out[...] = code((vel[0] + HALF * buoy * press[0]) * (TOP / W_MAX))
    b_out[...] = code((buoy - B_MID) * (TOP / B_MAX))
    loads[3].wait()
    pl.semaphore_wait(barrier, n_grp + 3)

    pending = []

    def send(src, dst, to, k):
        c = pltpu.make_async_remote_copy(
            src_ref=src, dst_ref=dst, send_sem=halo_send.at[k], recv_sem=halo_recv.at[k],
            device_id=(to, grp), device_id_type=MESH)
        c.start()
        pending.append(c)
        return c

    cells = [send(rcs.at[2], rcs.at[2 - d], near[d], i) for i, d in enumerate((-2, -1, 1, 2))]
    p0_down = send(p0_out, p0_in, below, 4)
    w_up = send(w_out, w_in, above, 5)
    b_up = send(b_out, b_in, above, 6)

    for c in loads[4:7]:
        c.wait()
    e_dev = obs.shape[0]
    eoff = pl.multiple_of(grp * e_dev, 128)
    wdev = weights[:, pl.ds(eoff, e_dev)].astype(F32)
    gdev = group[:, pl.ds(eoff, e_dev)]
    act_dev = jnp.where(
        gdev == lax.broadcasted_iota(I32, wdev.shape, 0), wdev, 0.0).astype(BF16)
    er = lax.broadcasted_iota(I32, (e_dev, e_dev * steps), 0)
    el = lax.broadcasted_iota(I32, (e_dev, e_dev * steps), 1)
    expand = jnp.where((el >> 2) == er, 1.0, 0.0).astype(BF16)
    wide = jnp.dot(act_dev, expand, preferred_element_type=F32).astype(BF16)
    rr = lax.broadcasted_iota(I32, (8 * n_grp, n_grp), 0)
    rl = lax.broadcasted_iota(I32, (8 * n_grp, n_grp), 1)
    rows = jnp.where((rr >> 3) == rl, 1.0, 0.0).astype(BF16)
    tall = jnp.dot(rows, wide, preferred_element_type=F32)
    tr = lax.broadcasted_iota(I32, tall.shape, 0)
    tl = lax.broadcasted_iota(I32, tall.shape, 1)
    lhs = jnp.where((tr & 7) == (tl & 3), tall, 0.0).astype(BF16)
    flat = obs[...].astype(F32).reshape(e_dev * steps, obs.shape[2]).astype(BF16)
    part = jnp.dot(lhs, flat, preferred_element_type=F32)
    encsend[...] = part.reshape(encsend.shape)
    enc_copies = []
    for d in range(1, n_grp):
        peer = lax.rem(grp + d, n_grp)
        c = pltpu.make_async_remote_copy(
            src_ref=encsend.at[peer], dst_ref=encrecv.at[d], send_sem=enc_send.at[d],
            recv_sem=enc_recv.at[d], device_id=(slab, peer), device_id_type=MESH)
        c.start()
        enc_copies.append(c)
    pending += enc_copies

    loads[7].wait()
    wall = weights[...].astype(F32)
    shot_row = lax.broadcasted_iota(I32, wall.shape, 0)
    own = jnp.sum(
        jnp.where((group[...] == shot_row) & (shot_row == grp), wall, 0.0),
        axis=0, keepdims=True)
    emit = wall.shape[1]
    ec = ecell[...] - slab * 65536
    ex = jnp.where((ec >= 0) & (ec < 65536), ec >> 8, -1)
    row_e = lax.broadcasted_iota(I32, (256, emit), 0)
    ax = jnp.where(row_e == ex, own, 0.0).astype(BF16)
    ay = jnp.where(row_e == (ec & 255), 1.0, 0.0).astype(BF16)
    amp = lax.dot_general(ax, ay, NT_DOT, preferred_element_type=F32)

    for c in cells:
        c.wait_recv()
    row_r = lax.broadcasted_iota(I32, (256, 128), 0)
    col_x, hot_y = {}, {}
    for d in range(-2, 3):
        rc = rcs[d + 2]
        inside = (slab + d >= 0) & (slab + d < n_slab)
        col_x[d] = jnp.where(inside, rc >> 8, -1000)
        y = jnp.where(inside, rc & 255, -1000)
        for dy in (-1, 0, 1) if abs(d) < 2 else (0,):
            hot_y[d, dy] = jnp.where(row_r == y + dy, 1.0, 0.0).astype(BF16)

    star = ((0, -1), (-1, 0), (0, 0), (1, 0), (0, 1))

    def spots(d, others):
        return [(d, dx, dy) for dx, dy in star] + [(o, 0, 0) for o in others]

    def blocks(points):
        return sorted({(d, dy) for d, _, dy in points})

    def gather(pieces, points):
        table = {}
        for key in blocks(points):
            table[key] = sum(
                jnp.dot(piece, hot_y[key], preferred_element_type=F32) for piece in pieces)
        return [
            jnp.sum(jnp.where(row_r == col_x[d] + dx, table[d, dy], 0.0), axis=0, keepdims=True)
            for d, dx, dy in points
        ]

    def scatter(values, points, split):
        left = []
        keys = blocks(points)
        for key in keys:
            total = 0.0
            for v, (d, dx, dy) in zip(values, points):
                if (d, dy) == key:
                    total = total + jnp.where(row_r == col_x[d] + dx, v, 0.0)
            left.append(total)
        right = [hot_y[key] for key in keys]
        pieces = [split(x) for x in left]
        count = len(pieces[0])
        lhs = jnp.concatenate([pc[i] for i in range(count) for pc in pieces], axis=1)
        rhs = jnp.concatenate(right * count, axis=1)
        return lax.dot_general(lhs, rhs, NT_DOT, preferred_element_type=F32)

    def column(rows_list):
        pad = 8 - len(rows_list)
        if pad:
            rows_list = rows_list + [jnp.zeros((pad, 128), F32)]
        return jnp.concatenate(rows_list, axis=0)

    only = [(0, 0, 0)]
    ring = spots(0, (1, -1))
    ones = jnp.ones((1, 128), F32)
    plain = lambda v: (v.astype(BF16),)
    count = scatter([ones] * 7, ring, plain)
    inv_ring = jnp.where(count > 0.5, 1.0 / count, 0.0)

    xi = lax.broadcasted_iota(I32, (256, 256), 0)
    yi = lax.broadcasted_iota(I32, (256, 256), 1)

    def up_x(f):
        return jnp.where(xi == 255, 0.0, pltpu.roll(f, 255, 0)) - f

    def up_y(f):
        return jnp.where(yi == 255, 0.0, pltpu.roll(f, 255, 1)) - f

    def down_x(f):
        return f - jnp.where(xi == 0, 0.0, pltpu.roll(f, 1, 0))

    def down_y(f):
        return f - jnp.where(yi == 0, 0.0, pltpu.roll(f, 1, 1))

    has_above = slab < n_slab - 1
    has_below = slab > 0
    for c in loads[8:]:
        c.wait()
    kappa = dens[...] * speed[...] * speed[...]
    keep = 1.0 - atten[...]
    hk = HALF * kappa
    hb = HALF * buoy

    def local_step(p, px, py):
        px = px - hb * up_x(p)
        py = py - hb * up_y(p)
        return px, py, down_x(px) + down_y(py)

    divs = [None] * steps
    recorded = [None] * steps
    p = press[0]
    px, py, flat_div = local_step(p, vel[1], vel[2])
    pz = vel[0] + hb * p
    base = keep * p + wav[0] * amp

    nearby = [(1, 0, 0), (-1, 0, 0)]
    kappa_at = gather(split2(kappa), spots(0, (1, -1)))
    buoy_at = gather(split2(buoy), [(0, 0, 0), (0, -1, 0), (0, 0, -1)] + nearby)
    keep_at = gather(split2(keep), only)[0]
    amp_at = gather(split3(amp), only)[0]

    p0_down.wait_recv()
    w_up.wait_recv()
    b_up.wait_recv()
    b_low = jnp.where(has_below, decode(b_in[...]) * (B_MAX / TOP) + B_MID, 0.0)
    hbl = HALF * b_low
    pzl = jnp.where(has_below, decode(w_in[...]) * (W_MAX / TOP), 0.0) - hbl * p
    pz = pz - hb * jnp.where(has_above, decode(p0_in[...]) * (P_MAX / TOP), 0.0)
    divs[0] = pz - pzl + flat_div
    p = base - hk * divs[0]
    press[1] = p

    top = jnp.maximum(top_of(p), 1e-30)
    p1_out[...] = code(p * (TOP / top))
    p1_scale[...] = jnp.broadcast_to(top * (1.0 / TOP), (8, 128))
    got = [
        send(p1_out, p1_in.at[0], below, 7), send(p1_out, p1_in.at[1], above, 8),
        send(p1_scale, p1_scale_in.at[0], below, 9),
        send(p1_scale, p1_scale_in.at[1], above, 10)]

    low_at = gather(split2(b_low), only + nearby)
    fix_out[...] = column([
        0.25 * kappa_at[5] * buoy_at[3], 0.25 * kappa_at[5] * low_at[1],
        0.25 * kappa_at[6] * buoy_at[4], 0.25 * kappa_at[6] * low_at[2]])
    fixed = [
        send(fix_out, fix_in.at[0], below, 11), send(fix_out, fix_in.at[1], above, 12)]
    k_at, b_at = kappa_at[2], buoy_at[0]
    own_at = 0.25 * k_at * b_at
    star_at = [
        kappa_at[0] * 0.25 * k_at * buoy_at[2],
        kappa_at[1] * 0.25 * k_at * buoy_at[1],
        k_at * (keep_at - 0.25 * k_at * (3.0 * b_at + buoy_at[1] + buoy_at[2] + low_at[0])),
        kappa_at[3] * own_at,
        kappa_at[4] * own_at]

    recorded[0] = gather(split3(p), only)[0]
    px, py, flat_div = local_step(p, px, py)
    pz = pz + hb * p
    pzl = pzl - hbl * p
    base = keep * p + wav[1] * amp
    for c in got:
        c.wait_recv()
    pz = pz - hb * jnp.where(has_above, decode(p1_in[0]) * p1_scale_in[0, 0:1, 0:1], 0.0)
    pzl = pzl + hbl * (decode(p1_in[1]) * p1_scale_in[1, 0:1, 0:1])
    divs[1] = pz - pzl + flat_div
    p = base - hk * divs[1]
    press[2] = p

    to_up, to_down = spots(1, (0, 2)), spots(-1, (0, -2))
    values = gather(split2(p), to_up + to_down)
    p2_out[0] = column(values[7:])
    p2_out[1] = column(values[:7])
    far_out[0] = column(values[13:])
    far_out[1] = column(values[6:7])
    got = [
        send(p2_out.at[0], p2_in.at[0], below, 13), send(p2_out.at[1], p2_in.at[1], above, 14)]
    far = [
        send(far_out.at[0], far_in.at[0], near[-2], 15),
        send(far_out.at[1], far_in.at[1], near[2], 16)]
    px, py, flat_div = local_step(p, px, py)
    pz = pz + hb * p
    pzl = pzl - hbl * p
    flat_div = pz - pzl + flat_div
    base = keep * p + wav[2] * amp - hk * flat_div
    values = gather(split2(base), nearby)
    part_out[0] = column(values[1:])
    part_out[1] = column(values[:1])
    parts = [
        send(part_out.at[0], part_in.at[0], below, 17),
        send(part_out.at[1], part_in.at[1], above, 18)]
    recorded[1] = gather(split3(p), only)[0]
    for c in got:
        c.wait_recv()
    ua = hb * (inv_ring * scatter(
        [p2_in[0, i:i + 1] for i in range(7)], spots(0, (1, -1)), split2))
    ub = hbl * (inv_ring * scatter(
        [p2_in[1, i:i + 1] for i in range(7)], spots(0, (-1, 1)), split2))
    pz = pz - ua
    pzl = pzl + ub
    divs[2] = flat_div - ua - ub
    p = base + hk * (ua + ub)
    press[3] = p
    recorded[2] = gather(split3(p), only)[0]

    px, py, flat_div = local_step(p, px, py)
    div_at = gather(split3(pz + hb * p - (pzl - hbl * p) + flat_div), only)[0]
    for c in far + fixed + parts:
        c.wait_recv()
    pa = part_in[0, 0:1] + fix_in[0, 2:3] * far_in[0, 0:1] + fix_in[0, 3:4] * recorded[1]
    pb = part_in[1, 0:1] + fix_in[1, 0:1] * recorded[1] + fix_in[1, 1:2] * far_in[1, 0:1]
    pa = jnp.where(has_above, pa, 0.0)
    div_at = div_at - HALF * (b_at * pa + low_at[0] * pb)
    recorded[3] = keep_at * recorded[2] - HALF * k_at * div_at + wav[3] * amp_at

    for c in enc_copies:
        c.wait_recv()
    enc = encsend[grp]
    for d in range(1, n_grp):
        enc = enc + encrecv[d]
    res = [(recorded[t] - enc[t:t + 1]) * (1.0 / n_grp) for t in range(steps)]

    sigma = k_at * res[3]
    star_rows = [v * res[3] for v in star_at]
    star_rows[2] = star_rows[2] + k_at * res[2]
    res_out[...] = column([sigma] + star_rows)
    got = [
        send(res_out, res_in.at[0], below, 19), send(res_out, res_in.at[1], above, 20),
        send(res_out, res_in.at[2], near[-2], 21), send(res_out, res_in.at[3], near[2], 22)]

    adj = scatter([res[3]], only, split3)
    gd = -adj * press[3]
    gk = scatter([-HALF * res[3] * div_at], only, split3)
    inj = [scatter([res[t]], only, split3) for t in range(steps - 1)]
    s = kappa * adj
    lz = -HALF * s
    lzl = HALF * s
    lx = HALF * up_x(s)
    ly = HALF * up_y(s)
    base = keep * adj + HALF * (down_x(buoy * lx) + down_y(buoy * ly)) + inj[2]
    for c in got:
        c.wait_recv()
    lz = lz + HALF * scatter([res_in[0, 0:1]], [(1, 0, 0)], split2)
    lzl = lzl - HALF * scatter([res_in[1, 0:1]], [(-1, 0, 0)], split2)
    adj = base + hb * lz - hbl * lzl
    sa = scatter(
        [res_in[0, i:i + 1] for i in range(1, 6)]
        + [fix_in[0, 0:1] * res_in[2, 0:1], fix_in[0, 3:4] * sigma],
        spots(1, (2, 0)), split2)
    sb = scatter(
        [res_in[1, i:i + 1] for i in range(1, 6)]
        + [fix_in[1, 0:1] * sigma, fix_in[1, 3:4] * res_in[3, 0:1]],
        spots(-1, (0, -2)), split2)
    gd = gd - adj * press[2]
    gk = gk - HALF * adj * divs[2]
    s = kappa * adj
    lz = lz + HALF * (sa - s)
    lzl = lzl + HALF * (s - sb)
    lx = lx + HALF * up_x(s)
    ly = ly + HALF * up_y(s)
    adj = inj[1] + keep * adj + (
        hb * lz - hbl * lzl + HALF * (down_x(buoy * lx) + down_y(buoy * ly)))
    s = kappa * adj
    top = jnp.maximum(top_of(s), 1e-30)
    s1_out[...] = code_root(s, top)
    s1_scale[...] = jnp.broadcast_to(top * (1.0 / (TOP * TOP)), (8, 128))
    got = [
        send(s1_out, s1_in.at[0], below, 23), send(s1_out, s1_in.at[1], above, 24),
        send(s1_scale, s1_scale_in.at[0], below, 25),
        send(s1_scale, s1_scale_in.at[1], above, 26)]
    gd = gd - adj * press[1]
    gk = gk - HALF * adj * divs[1]
    lz = lz - HALF * s
    lzl = lzl + HALF * s
    lx = lx + HALF * up_x(s)
    ly = ly + HALF * up_y(s)
    adj = inj[0] + keep * adj + (
        hb * lz - hbl * lzl + HALF * (down_x(buoy * lx) + down_y(buoy * ly)))
    for c in got:
        c.wait_recv()
    sa = jnp.where(has_above, decode_root(s1_in[0]) * s1_scale_in[0, 0:1, 0:1], 0.0)
    sb = decode_root(s1_in[1]) * s1_scale_in[1, 0:1, 0:1]
    adj = adj + HALF * (hb * sa + hbl * sb)
    gd = gd - adj * press[0]
    gk = gk - HALF * adj * divs[0]
    gk = gk * (2.0 * dens[...] * speed[...])
    for i, g in enumerate((gk, gd)):
        grad[i] = g
        top = jnp.maximum(top_of(g), 1e-30)
        coded[i] = code_root(g, top)
        gscale[i] = jnp.broadcast_to(top * (1.0 / (TOP * TOP)), (8, 128))
    rows_out = 256 // n_grp
    copies = []
    for d in range(1, n_grp):
        peer = lax.rem(grp + d, n_grp)
        c = pltpu.make_async_remote_copy(
            src_ref=coded.at[:, pl.ds(pl.multiple_of(peer * rows_out, rows_out), rows_out)],
            dst_ref=gradrecv.at[d], send_sem=grad_send.at[d],
            recv_sem=grad_recv.at[d], device_id=(slab, peer), device_id_type=MESH)
        c.start()
        e = pltpu.make_async_remote_copy(
            src_ref=gscale, dst_ref=gscale_in.at[d], send_sem=gs_send.at[d],
            recv_sem=gs_recv.at[d], device_id=(slab, peer), device_id_type=MESH)
        e.start()
        copies.append((c, e))
    mine = pl.ds(pl.multiple_of(grp * rows_out, rows_out), rows_out)
    total = [grad[0, mine], grad[1, mine]]
    for d in range(1, n_grp):
        for c in copies[d - 1]:
            c.wait_recv()
        for i in range(2):
            total[i] = total[i] + decode_root(gradrecv[d, i]) * gscale_in[d, i, 0:1, 0:1]
    out_s[0] = total[0]
    out_a[0] = total[1]
    for c in pending + [c for pair in copies for c in pair]:
        c.wait_send()


def shards(
    n_slab, n_grp,
    sound_speed, density, attenuation, wavelet, weights, emitter_group, emitter_cell,
    receiver_cell, pressure_start, velocity_start, observed,
):
    vmem = pl.BlockSpec(memory_space=pltpu.VMEM)
    hbm = pl.BlockSpec(memory_space=pltpu.HBM)
    smem = pl.BlockSpec(memory_space=pltpu.SMEM)
    rows = 256 // n_grp
    plane = lambda *n, t=F32: pltpu.VMEM(n + (256, 256), t)
    tile = lambda *n: pltpu.VMEM(n + (8, 128), F32)
    out = jax.ShapeDtypeStruct((1, rows, 256), F32)
    dma = pltpu.SemaphoreType.DMA
    emit = weights.shape[1]
    return pl.pallas_call(
        functools.partial(kernel, n_slab, n_grp),
        out_shape=(out, out),
        in_specs=[smem] + [hbm] * 10,
        out_specs=(vmem, vmem),
        scratch_shapes=[
            plane(), plane(), plane(), plane(4), plane(3),
            pltpu.VMEM(weights.shape, BF16), pltpu.VMEM((1, emit), I32),
            pltpu.VMEM((1, emit), I32), pltpu.VMEM(observed.shape, BF16),
            pltpu.VMEM((5, 1, 128), I32),
            plane(t=I16), plane(t=I16), plane(t=I16), plane(t=I16), plane(t=I16),
            plane(t=I16), plane(t=I16), plane(t=I16), plane(2, t=I16), plane(2, t=I16),
            tile(), tile(2), tile(2), tile(2), tile(2), tile(2), tile(2), tile(2), tile(), tile(2),
            tile(), tile(4), tile(), tile(2),
            tile(n_grp), tile(n_grp), plane(2), plane(2, t=I16),
            pltpu.VMEM((n_grp, 2, rows, 256), I16), tile(2), tile(n_grp, 2),
            dma((10,)), dma((27,)), dma((27,)), dma((n_grp,)), dma((n_grp,)),
            dma((n_grp,)), dma((n_grp,)), dma((n_grp,)), dma((n_grp,)),
        ],
        compiler_params=pltpu.CompilerParams(
            collective_id=0, has_side_effects=True, vmem_limit_bytes=60 * 1024 * 1024),
    )(
        wavelet, sound_speed, density, attenuation, pressure_start, velocity_start, weights,
        emitter_group.reshape(1, -1), emitter_cell.reshape(1, -1),
        receiver_cell.reshape(1, -1), observed,
    )


def solution(mesh):
    return jax.shard_map(
        functools.partial(shards, mesh.shape["slab"], mesh.shape["grp"]),
        mesh=mesh,
        in_specs=(
            P("slab", None, None),
            P("slab", None, None),
            P("slab", None, None),
            P(),
            P(),
            P(),
            P(),
            P("slab"),
            P("grp", "slab", None, None),
            P(None, "grp", "slab", None, None),
            P("grp", None, "slab"),
        ),
        out_specs=(P("slab", "grp", None), P("slab", "grp", None)),
        check_vma=False,
    )
```

time: 104 us -> 61 us (0.59)
  Pallas kernels: 93.3 us -> 58.1 us
  local copies, waits for them, and re-layouts: 9.14 us -> 2 us
    pallas_call x1, Pallas kernels: 93.3 us -> 58.1 us  [shards(): pl.pallas_call(functools.partial(kernel, n_slab, n_grp), out_shape=(out,...]
    unnamed x24 -> x4, local copies, waits for them, and re-layouts: 9.14 us -> 2 us
where the time goes in v2:
time: 61 us; the launch traced here: 60.7 us
  Pallas kernels  58.1 us (95%)
  local copies, waits for them, and re-layouts  2 us (3%)
  between operations  0.65 us (1%)
    pallas_call x1, Pallas kernels, shards(): pl.pallas_call(functools.partial(kernel, n_slab, n_grp), out_shape=(out,...  58.1 us
    unnamed x4, local copies, waits for them, and re-layouts  2 us

profile of v2, /device:TPU:6, one launch (start us, length us, event | category | flops | bytes accessed | tf_op | source)
XLA Modules:
  0.0 60.7 jit_solution(1559701914891861955)
XLA Ops:
  0.6 58.1 %shard_map.122 = (f32[1,32,256]{2,1,0:T(8,128)}, f32[1,32,256]{2,1,0:T(8,128)}) custom-call(f32[4]{0:T(128)} %wav.1, f32[1,256,256]{2,1,0:T(8,128)} %speed_h.1, f32[1,256,256]{2,1,0:T(8,128)} %dens_h.1, f32[1,256,256]{2,1,0:T(8,128)} %atten_h.1, f32[1,1,256,256]{3,2,1,0:T(8,128)} %press_h.1, f32[3,1,1,256,256]{4,3,2,1,0:T(8,128)} %vel_h.1, ...), custom_call_target="tpu_custom_call" | custom-call | tf_op jit(solution)/shard_map/pallas_call | solution.py:478
  58.7 0.0 copy-start
  58.7 1.4 %copy.15 = f32[1,32,256]{2,1,0:T(8,128)} copy(f32[1,32,256]{2,1,0:T(8,128)} %get-tuple-element.4) | data formatting | bytes 65536
  60.1 0.0 copy-done
  60.1 0.6 %copy.16 = f32[1,32,256]{2,1,0:T(8,128)} copy(f32[1,32,256]{2,1,0:T(8,128)S(1)} %copy-done) | data formatting | bytes 65536
Async XLA Ops:
  58.7 1.4 %copy-start = (f32[1,32,256]{2,1,0:T(8,128)S(1)}, f32[1,32,256]{2,1,0:T(8,128)}, u32[]{:S(2)}) copy-start(f32[1,32,256]{2,1,0:T(8,128)} %get-tuple-element.5) | copy-start | bytes 98308

commit v3 on v2

--- a/solution.py
+++ b/solution.py
@@ -56,6 +56,10 @@
 W_MAX = 7.3
 B_MID = 1.0714286
 B_MAX = 0.3573
+K_MID = 0.7875
+K_MAX = 0.6127
+D_MID = 0.895
+D_MAX = 0.0952
 
 
 def kernel(
@@ -63,9 +67,9 @@
     wav, speed_h, dens_h, atten_h, press_h, vel_h, weights_h, group_h, ecell_h, rcell_h, obs_h,
     out_s, out_a,
     speed, dens, atten, press, vel, weights, group, ecell, obs, rcs,
-    p0_out, w_out, b_out, p1_out, s1_out, p0_in, w_in, b_in, p1_in, s1_in,
+    p0_out, w_out, b_out, p1_out, p0_in, w_in, b_in, p1_in,
     p1_scale, p1_scale_in, p2_out, p2_in, far_out, far_in, part_out, part_in, fix_out, fix_in,
-    res_out, res_in, s1_scale, s1_scale_in,
+    res_out, res_in, fix2_in, k_out, k_in, d_out, d_in, b2_in,
     encsend, encrecv, grad, coded, gradrecv, gscale, gscale_in,
     load_sem, halo_send, halo_recv, enc_send, enc_recv, grad_send, grad_recv, gs_send, gs_recv,
 ):
@@ -79,14 +83,14 @@
         pltpu.make_async_copy(src, dst, load_sem.at[i])
         for i, (src, dst) in enumerate([
             (press_h.at[0, 0], press.at[0]), (dens_h.at[0], dens), (vel_h.at[:, 0, 0], vel),
-            (rcell_h, rcs.at[2]), (weights_h, weights), (group_h, group), (obs_h, obs),
+            (rcell_h, rcs.at[3]), (weights_h, weights), (group_h, group), (obs_h, obs),
             (ecell_h, ecell), (speed_h.at[0], speed), (atten_h.at[0], atten),
         ])
     ]
     for c in loads:
         c.start()
 
-    near = {d: lax.rem(slab + n_slab + d, n_slab) for d in (-2, -1, 1, 2)}
+    near = {d: lax.rem(slab + n_slab + d, n_slab) for d in (-3, -2, -1, 1, 2, 3)}
     barrier = pltpu.get_barrier_semaphore()
     for s in near.values():
         pl.semaphore_signal(barrier, inc=1, device_id=(s, grp), device_id_type=MESH)
@@ -101,7 +105,7 @@
     w_out[...] = code((vel[0] + HALF * buoy * press[0]) * (TOP / W_MAX))
     b_out[...] = code((buoy - B_MID) * (TOP / B_MAX))
     loads[3].wait()
-    pl.semaphore_wait(barrier, n_grp + 3)
+    pl.semaphore_wait(barrier, n_grp + 5)
 
     pending = []
 
@@ -113,7 +117,7 @@
         pending.append(c)
         return c
 
-    cells = [send(rcs.at[2], rcs.at[2 - d], near[d], i) for i, d in enumerate((-2, -1, 1, 2))]
+    cells = [send(rcs.at[3], rcs.at[3 - d], near[d], 27 + d) for d in near]
     p0_down = send(p0_out, p0_in, below, 4)
     w_up = send(w_out, w_in, above, 5)
     b_up = send(b_out, b_in, above, 6)
@@ -168,12 +172,12 @@
         c.wait_recv()
     row_r = lax.broadcasted_iota(I32, (256, 128), 0)
     col_x, hot_y = {}, {}
-    for d in range(-2, 3):
-        rc = rcs[d + 2]
+    for d in range(-3, 4):
+        rc = rcs[d + 3]
         inside = (slab + d >= 0) & (slab + d < n_slab)
         col_x[d] = jnp.where(inside, rc >> 8, -1000)
         y = jnp.where(inside, rc & 255, -1000)
-        for dy in (-1, 0, 1) if abs(d) < 2 else (0,):
+        for dy in (-1, 0, 1) if abs(d) < 3 else (0,):
             hot_y[d, dy] = jnp.where(row_r == y + dy, 1.0, 0.0).astype(BF16)
 
     star = ((0, -1), (-1, 0), (0, 0), (1, 0), (0, 1))
@@ -284,12 +288,18 @@
         send(p1_scale, p1_scale_in.at[0], below, 9),
         send(p1_scale, p1_scale_in.at[1], above, 10)]
 
+    k_out[...] = code((kappa - K_MID) * (TOP / K_MAX))
+    d_out[...] = code((keep - D_MID) * (TOP / D_MAX))
+    planes = [
+        send(k_out, k_in.at[0], below, 0), send(k_out, k_in.at[1], above, 1),
+        send(d_out, d_in.at[0], below, 2), send(d_out, d_in.at[1], above, 3)]
     low_at = gather(split2(b_low), only + nearby)
     fix_out[...] = column([
         0.25 * kappa_at[5] * buoy_at[3], 0.25 * kappa_at[5] * low_at[1],
         0.25 * kappa_at[6] * buoy_at[4], 0.25 * kappa_at[6] * low_at[2]])
     fixed = [
-        send(fix_out, fix_in.at[0], below, 11), send(fix_out, fix_in.at[1], above, 12)]
+        send(fix_out, fix_in.at[0], below, 11), send(fix_out, fix_in.at[1], above, 12),
+        send(fix_out, fix2_in.at[0], near[-2], 31), send(fix_out, fix2_in.at[1], near[2], 32)]
     k_at, b_at = kappa_at[2], buoy_at[0]
     own_at = 0.25 * k_at * b_at
     star_at = [
@@ -323,6 +333,7 @@
     far = [
         send(far_out.at[0], far_in.at[0], near[-2], 15),
         send(far_out.at[1], far_in.at[1], near[2], 16)]
+    planes += [send(b_out, b2_in.at[0], below, 33), send(b_out, b2_in.at[1], near[2], 34)]
     px, py, flat_div = local_step(p, px, py)
     pz = pz + hb * p
     pzl = pzl - hbl * p
@@ -368,64 +379,67 @@
     sigma = k_at * res[3]
     star_rows = [v * res[3] for v in star_at]
     star_rows[2] = star_rows[2] + k_at * res[2]
-    res_out[...] = column([sigma] + star_rows)
+    res_out[...] = column([sigma] + star_rows + [k_at * res[1]])
     got = [
         send(res_out, res_in.at[0], below, 19), send(res_out, res_in.at[1], above, 20),
-        send(res_out, res_in.at[2], near[-2], 21), send(res_out, res_in.at[3], near[2], 22)]
-
+        send(res_out, res_in.at[2], near[-2], 21), send(res_out, res_in.at[3], near[2], 22),
+        send(res_out, res_in.at[4], near[-3], 23), send(res_out, res_in.at[5], near[3], 20 + 15)]
+
+    def spread(b, f):
+        return down_x(b * up_x(f)) + down_y(b * up_y(f))
+
+    qb = 0.25 * buoy
+    qbl = 0.25 * b_low
     adj = scatter([res[3]], only, split3)
     gd = -adj * press[3]
     gk = scatter([-HALF * res[3] * div_at], only, split3)
     inj = [scatter([res[t]], only, split3) for t in range(steps - 1)]
-    s = kappa * adj
-    lz = -HALF * s
-    lzl = HALF * s
-    lx = HALF * up_x(s)
-    ly = HALF * up_y(s)
-    base = keep * adj + HALF * (down_x(buoy * lx) + down_y(buoy * ly)) + inj[2]
+    total = kappa * adj
+    base = inj[2] + keep * adj + spread(qb, total) - (qb + qbl) * total
+    for c in planes:
+        c.wait_recv()
+    k_near = [decode(k_in[i]) * (K_MAX / TOP) + K_MID for i in range(2)]
+    d_near = [decode(d_in[i]) * (D_MAX / TOP) + D_MID for i in range(2)]
+    k_near[0] = jnp.where(has_above, k_near[0], 0.0)
+    b_near = [decode(b2_in[i]) * (B_MAX * 0.25 / TOP) + B_MID * 0.25 for i in range(2)]
+    b_near[1] = jnp.where(slab > 1, b_near[1], 0.0)
     for c in got:
         c.wait_recv()
-    lz = lz + HALF * scatter([res_in[0, 0:1]], [(1, 0, 0)], split2)
-    lzl = lzl - HALF * scatter([res_in[1, 0:1]], [(-1, 0, 0)], split2)
-    adj = base + hb * lz - hbl * lzl
-    sa = scatter(
-        [res_in[0, i:i + 1] for i in range(1, 6)]
-        + [fix_in[0, 0:1] * res_in[2, 0:1], fix_in[0, 3:4] * sigma],
-        spots(1, (2, 0)), split2)
-    sb = scatter(
-        [res_in[1, i:i + 1] for i in range(1, 6)]
-        + [fix_in[1, 0:1] * sigma, fix_in[1, 3:4] * res_in[3, 0:1]],
-        spots(-1, (0, -2)), split2)
+
+    def row(i, k):
+        return res_in[i, k:k + 1]
+
+    last, second, outer, first = [], [], [], []
+    for i, d in enumerate((1, -1)):
+        up, down = (fix_in[i, 0:1], fix_in[i, 3:4])
+        up2, down2 = (fix2_in[i, 0:1], fix2_in[i, 3:4])
+        out_row, in_row, out2, in2 = (up, down, up2, down2) if d > 0 else (down, up, down2, up2)
+        last.append(scatter([row(i, 0)], [(d, 0, 0)], split2))
+        first.append(scatter([row(i, 6)], [(d, 0, 0)], split2))
+        second.append(scatter(
+            [row(i, k) for k in range(1, 6)] + [out_row * row(i + 2, 0), in_row * sigma],
+            spots(d, (2 * d, 0)), split2))
+        rows_far = [row(i + 2, k) for k in range(1, 6)]
+        rows_far[2] = rows_far[2] + row(i + 2, 0)
+        outer.append(scatter(
+            rows_far + [out2 * row(i + 4, 0), in2 * row(i, 0)],
+            spots(2 * d, (3 * d, d)), split2))
+    adj = base + qb * last[0] + qbl * last[1]
     gd = gd - adj * press[2]
     gk = gk - HALF * adj * divs[2]
-    s = kappa * adj
-    lz = lz + HALF * (sa - s)
-    lzl = lzl + HALF * (s - sb)
-    lx = lx + HALF * up_x(s)
-    ly = ly + HALF * up_y(s)
-    adj = inj[1] + keep * adj + (
-        hb * lz - hbl * lzl + HALF * (down_x(buoy * lx) + down_y(buoy * ly)))
-    s = kappa * adj
-    top = jnp.maximum(top_of(s), 1e-30)
-    s1_out[...] = code_root(s, top)
-    s1_scale[...] = jnp.broadcast_to(top * (1.0 / (TOP * TOP)), (8, 128))
-    got = [
-        send(s1_out, s1_in.at[0], below, 23), send(s1_out, s1_in.at[1], above, 24),
-        send(s1_scale, s1_scale_in.at[0], below, 25),
-        send(s1_scale, s1_scale_in.at[1], above, 26)]
+    total = total + kappa * adj
+    both = [last[i] + second[i] for i in range(2)]
+    sa = first[0] + d_near[0] * second[0] + k_near[0] * (
+        spread(b_near[0], both[0]) + b_near[0] * (outer[0] - both[0]) + qb * (total - both[0]))
+    sb = first[1] + d_near[1] * second[1] + k_near[1] * (
+        spread(qbl, both[1]) + qbl * (total - both[1]) + b_near[1] * (outer[1] - both[1]))
+    adj = inj[1] + keep * adj + spread(qb, total) + (
+        qb * (both[0] - total) + qbl * (both[1] - total))
     gd = gd - adj * press[1]
     gk = gk - HALF * adj * divs[1]
-    lz = lz - HALF * s
-    lzl = lzl + HALF * s
-    lx = lx + HALF * up_x(s)
-    ly = ly + HALF * up_y(s)
-    adj = inj[0] + keep * adj + (
-        hb * lz - hbl * lzl + HALF * (down_x(buoy * lx) + down_y(buoy * ly)))
-    for c in got:
-        c.wait_recv()
-    sa = jnp.where(has_above, decode_root(s1_in[0]) * s1_scale_in[0, 0:1, 0:1], 0.0)
-    sb = decode_root(s1_in[1]) * s1_scale_in[1, 0:1, 0:1]
-    adj = adj + HALF * (hb * sa + hbl * sb)
+    total = total + kappa * adj
+    adj = inj[0] + keep * adj + spread(qb, total) + (
+        qb * (both[0] + sa - total) + qbl * (both[1] + sb - total))
     gd = gd - adj * press[0]
     gk = gk - HALF * adj * divs[0]
     gk = gk * (2.0 * dens[...] * speed[...])
@@ -484,14 +498,15 @@
             plane(), plane(), plane(), plane(4), plane(3),
             pltpu.VMEM(weights.shape, BF16), pltpu.VMEM((1, emit), I32),
             pltpu.VMEM((1, emit), I32), pltpu.VMEM(observed.shape, BF16),
-            pltpu.VMEM((5, 1, 128), I32),
-            plane(t=I16), plane(t=I16), plane(t=I16), plane(t=I16), plane(t=I16),
-            plane(t=I16), plane(t=I16), plane(t=I16), plane(2, t=I16), plane(2, t=I16),
+            pltpu.VMEM((7, 1, 128), I32),
+            plane(t=I16), plane(t=I16), plane(t=I16), plane(t=I16),
+            plane(t=I16), plane(t=I16), plane(t=I16), plane(2, t=I16),
             tile(), tile(2), tile(2), tile(2), tile(2), tile(2), tile(2), tile(2), tile(), tile(2),
-            tile(), tile(4), tile(), tile(2),
+            tile(), tile(6), tile(2), plane(t=I16), plane(2, t=I16), plane(t=I16),
+            plane(2, t=I16), plane(2, t=I16),
             tile(n_grp), tile(n_grp), plane(2), plane(2, t=I16),
             pltpu.VMEM((n_grp, 2, rows, 256), I16), tile(2), tile(n_grp, 2),
-            dma((10,)), dma((27,)), dma((27,)), dma((n_grp,)), dma((n_grp,)),
+            dma((10,)), dma((36,)), dma((36,)), dma((n_grp,)), dma((n_grp,)),
             dma((n_grp,)), dma((n_grp,)), dma((n_grp,)), dma((n_grp,)),
         ],
         compiler_params=pltpu.CompilerParams(

time: 61 us -> 59.6 us (0.977)
  Pallas kernels: 58.1 us -> 56.7 us
    pallas_call x1, Pallas kernels: 58.1 us -> 56.7 us  [shards(): pl.pallas_call(functools.partial(kernel, n_slab, n_grp), out_shape=(out,...]
where the time goes in v3:
time: 59.6 us; the launch traced here: 59.4 us
  Pallas kernels  56.7 us (95%)
  local copies, waits for them, and re-layouts  2 us (3%)
  between operations  0.65 us (1%)
    pallas_call x1, Pallas kernels, shards(): pl.pallas_call(functools.partial(kernel, n_slab, n_grp), out_shape=(out,...  56.7 us
    unnamed x4, local copies, waits for them, and re-layouts  2 us

profile of v3, /device:TPU:6, one launch (start us, length us, event | category | flops | bytes accessed | tf_op | source)
XLA Modules:
  0.0 59.4 jit_solution(15516663678680672904)
XLA Ops:
  0.6 56.7 %shard_map.122 = (f32[1,32,256]{2,1,0:T(8,128)}, f32[1,32,256]{2,1,0:T(8,128)}) custom-call(f32[4]{0:T(128)} %wav.1, f32[1,256,256]{2,1,0:T(8,128)} %speed_h.1, f32[1,256,256]{2,1,0:T(8,128)} %dens_h.1, f32[1,256,256]{2,1,0:T(8,128)} %atten_h.1, f32[1,1,256,256]{3,2,1,0:T(8,128)} %press_h.1, f32[3,1,1,256,256]{4,3,2,1,0:T(8,128)} %vel_h.1, ...), custom_call_target="tpu_custom_call" | custom-call | tf_op jit(solution)/shard_map/pallas_call | solution.py:492
  57.4 0.0 copy-start
  57.4 1.4 %copy.15 = f32[1,32,256]{2,1,0:T(8,128)} copy(f32[1,32,256]{2,1,0:T(8,128)} %get-tuple-element.4) | data formatting | bytes 65536
  58.8 0.0 copy-done
  58.8 0.6 %copy.16 = f32[1,32,256]{2,1,0:T(8,128)} copy(f32[1,32,256]{2,1,0:T(8,128)S(1)} %copy-done) | data formatting | bytes 65536
Async XLA Ops:
  57.4 1.4 %copy-start = (f32[1,32,256]{2,1,0:T(8,128)S(1)}, f32[1,32,256]{2,1,0:T(8,128)}, u32[]{:S(2)}) copy-start(f32[1,32,256]{2,1,0:T(8,128)} %get-tuple-element.5) | copy-start | bytes 98308

commit v4 on v3

--- a/solution.py
+++ b/solution.py
@@ -54,6 +54,7 @@
 
 P_MAX = 6.0
 W_MAX = 7.3
+V_MAX = 11.6
 B_MID = 1.0714286
 B_MAX = 0.3573
 K_MID = 0.7875
@@ -65,7 +66,7 @@
 def kernel(
     n_slab, n_grp,
     wav, speed_h, dens_h, atten_h, press_h, vel_h, weights_h, group_h, ecell_h, rcell_h, obs_h,
-    out_s, out_a,
+    out,
     speed, dens, atten, press, vel, weights, group, ecell, obs, rcs,
     p0_out, w_out, b_out, p1_out, p0_in, w_in, b_in, p1_in,
     p1_scale, p1_scale_in, p2_out, p2_in, far_out, far_in, part_out, part_in, fix_out, fix_in,
@@ -189,10 +190,12 @@
         return sorted({(d, dy) for d, _, dy in points})
 
     def gather(pieces, points):
-        table = {}
-        for key in blocks(points):
-            table[key] = sum(
-                jnp.dot(piece, hot_y[key], preferred_element_type=F32) for piece in pieces)
+        keys = blocks(points)
+        wide = jnp.concatenate([hot_y[key] for key in keys], axis=1)
+        values = jnp.dot(
+            jnp.concatenate(pieces, axis=1), jnp.concatenate([wide] * len(pieces), axis=0),
+            preferred_element_type=F32)
+        table = {key: values[:, i * 128:(i + 1) * 128] for i, key in enumerate(keys)}
         return [
             jnp.sum(jnp.where(row_r == col_x[d] + dx, table[d, dy], 0.0), axis=0, keepdims=True)
             for d, dx, dy in points
@@ -262,12 +265,18 @@
     px, py, flat_div = local_step(p, vel[1], vel[2])
     pz = vel[0] + hb * p
     base = keep * p + wav[0] * amp
+    top = 1.001 * (
+        top_of(base - hk * (pz + flat_div)) + P_MAX * top_of(hk * hb) + V_MAX * top_of(hk))
+    p1_scale[...] = jnp.broadcast_to(top * (1.0 / TOP), (8, 128))
+    got = [
+        send(p1_scale, p1_scale_in.at[0], below, 9), send(p1_scale, p1_scale_in.at[1], above, 10)]
+    to_code = TOP / top
 
     nearby = [(1, 0, 0), (-1, 0, 0)]
     kappa_at = gather(split2(kappa), spots(0, (1, -1)))
     buoy_at = gather(split2(buoy), [(0, 0, 0), (0, -1, 0), (0, 0, -1)] + nearby)
     keep_at = gather(split2(keep), only)[0]
-    amp_at = gather(split3(amp), only)[0]
+    amp_at = gather(split2(amp), only)[0]
 
     p0_down.wait_recv()
     w_up.wait_recv()
@@ -280,13 +289,8 @@
     p = base - hk * divs[0]
     press[1] = p
 
-    top = jnp.maximum(top_of(p), 1e-30)
-    p1_out[...] = code(p * (TOP / top))
-    p1_scale[...] = jnp.broadcast_to(top * (1.0 / TOP), (8, 128))
-    got = [
-        send(p1_out, p1_in.at[0], below, 7), send(p1_out, p1_in.at[1], above, 8),
-        send(p1_scale, p1_scale_in.at[0], below, 9),
-        send(p1_scale, p1_scale_in.at[1], above, 10)]
+    p1_out[...] = code(p * to_code)
+    got += [send(p1_out, p1_in.at[0], below, 7), send(p1_out, p1_in.at[1], above, 8)]
 
     k_out[...] = code((kappa - K_MID) * (TOP / K_MAX))
     d_out[...] = code((keep - D_MID) * (TOP / D_MAX))
@@ -309,7 +313,7 @@
         kappa_at[3] * own_at,
         kappa_at[4] * own_at]
 
-    recorded[0] = gather(split3(p), only)[0]
+    recorded[0] = gather(split2(p), only)[0]
     px, py, flat_div = local_step(p, px, py)
     pz = pz + hb * p
     pzl = pzl - hbl * p
@@ -345,7 +349,7 @@
     parts = [
         send(part_out.at[0], part_in.at[0], below, 17),
         send(part_out.at[1], part_in.at[1], above, 18)]
-    recorded[1] = gather(split3(p), only)[0]
+    recorded[1] = gather(split2(p), only)[0]
     for c in got:
         c.wait_recv()
     ua = hb * (inv_ring * scatter(
@@ -357,10 +361,10 @@
     divs[2] = flat_div - ua - ub
     p = base + hk * (ua + ub)
     press[3] = p
-    recorded[2] = gather(split3(p), only)[0]
+    recorded[2] = gather(split2(p), only)[0]
 
     px, py, flat_div = local_step(p, px, py)
-    div_at = gather(split3(pz + hb * p - (pzl - hbl * p) + flat_div), only)[0]
+    div_at = gather(split2(pz + hb * p - (pzl - hbl * p) + flat_div), only)[0]
     for c in far + fixed + parts:
         c.wait_recv()
     pa = part_in[0, 0:1] + fix_in[0, 2:3] * far_in[0, 0:1] + fix_in[0, 3:4] * recorded[1]
@@ -469,8 +473,8 @@
             c.wait_recv()
         for i in range(2):
             total[i] = total[i] + decode_root(gradrecv[d, i]) * gscale_in[d, i, 0:1, 0:1]
-    out_s[0] = total[0]
-    out_a[0] = total[1]
+    out[0] = total[0]
+    out[1] = total[1]
     for c in pending + [c for pair in copies for c in pair]:
         c.wait_send()
 
@@ -486,14 +490,14 @@
     rows = 256 // n_grp
     plane = lambda *n, t=F32: pltpu.VMEM(n + (256, 256), t)
     tile = lambda *n: pltpu.VMEM(n + (8, 128), F32)
-    out = jax.ShapeDtypeStruct((1, rows, 256), F32)
+    out = jax.ShapeDtypeStruct((2, rows, 256), F32)
     dma = pltpu.SemaphoreType.DMA
     emit = weights.shape[1]
-    return pl.pallas_call(
+    both = pl.pallas_call(
         functools.partial(kernel, n_slab, n_grp),
-        out_shape=(out, out),
+        out_shape=out,
         in_specs=[smem] + [hbm] * 10,
-        out_specs=(vmem, vmem),
+        out_specs=vmem,
         scratch_shapes=[
             plane(), plane(), plane(), plane(4), plane(3),
             pltpu.VMEM(weights.shape, BF16), pltpu.VMEM((1, emit), I32),
@@ -516,6 +520,7 @@
         emitter_group.reshape(1, -1), emitter_cell.reshape(1, -1),
         receiver_cell.reshape(1, -1), observed,
     )
+    return both[0:1], both[1:2]
 
 
 def solution(mesh):

time: 59.6 us -> 58.7 us (0.985)
  local copies, waits for them, and re-layouts: 2 us -> 1.4 us
    unnamed x4 -> x0, local copies, waits for them, and re-layouts: 2 us -> none
    slice x0 -> x1, local copies, waits for them, and re-layouts: none -> 1.4 us  [shards(): return (both[0:1], both[1:2])]
where the time goes in v4:
time: 58.7 us; the launch traced here: 58.5 us
  Pallas kernels  56.4 us (96%)
  local copies, waits for them, and re-layouts  1.4 us (2%)
  between operations  0.64 us (1%)
    pallas_call x1, Pallas kernels, shards(): pl.pallas_call(functools.partial(kernel, n_slab, n_grp), out_shape=out, i...  56.4 us
    slice x1, local copies, waits for them, and re-layouts, shards(): return (both[0:1], both[1:2])  1.4 us

profile of v4, /device:TPU:6, one launch (start us, length us, event | category | flops | bytes accessed | tf_op | source)
XLA Modules:
  0.0 58.5 jit_solution(12562705695243784518)
XLA Ops:
  0.6 56.4 %shard_map.122 = f32[2,32,256]{2,1,0:T(8,128)} custom-call(f32[4]{0:T(128)} %wav.1, f32[1,256,256]{2,1,0:T(8,128)} %speed_h.1, f32[1,256,256]{2,1,0:T(8,128)} %dens_h.1, f32[1,256,256]{2,1,0:T(8,128)} %atten_h.1, f32[1,1,256,256]{3,2,1,0:T(8,128)} %press_h.1, f32[3,1,1,256,256]{4,3,2,1,0:T(8,128)} %vel_h.1, bf16[8,1024]{1,0:T(8,128)(2,1)} %weights_h.1, ...), custom_call_target="tpu_custom_call" | custom-call | tf_op jit(solution)/shard_map/pallas_call | solution.py:496
  57.1 1.4 %fusion = (f32[1,32,256]{2,1,0:T(8,128)}, f32[1,32,256]{2,1,0:T(8,128)}) fusion(f32[2,32,256]{2,1,0:T(8,128)} %shard_map.122), kind=kLoop, calls=%fused_computation | loop fusion | bytes 131072 | tf_op jit(solution)/shard_map/slice | solution.py:523

commit v5 on v4

--- a/solution.py
+++ b/solution.py
@@ -68,9 +68,9 @@
     wav, speed_h, dens_h, atten_h, press_h, vel_h, weights_h, group_h, ecell_h, rcell_h, obs_h,
     out,
     speed, dens, atten, press, vel, weights, group, ecell, obs, rcs,
-    p0_out, w_out, b_out, p1_out, p0_in, w_in, b_in, p1_in,
+    p0_out, w_out, p1_out, p0_in, w_in, b_in, p1_in,
     p1_scale, p1_scale_in, p2_out, p2_in, far_out, far_in, part_out, part_in, fix_out, fix_in,
-    res_out, res_in, fix2_in, k_out, k_in, d_out, d_in, b2_in,
+    res_out, res_in, fix2_in, near_out, near_in,
     encsend, encrecv, grad, coded, gradrecv, gscale, gscale_in,
     load_sem, halo_send, halo_recv, enc_send, enc_recv, grad_send, grad_recv, gs_send, gs_recv,
 ):
@@ -104,25 +104,7 @@
     p0_out[...] = code(press[0] * (TOP / P_MAX))
     buoy = 1.0 / dens[...]
     w_out[...] = code((vel[0] + HALF * buoy * press[0]) * (TOP / W_MAX))
-    b_out[...] = code((buoy - B_MID) * (TOP / B_MAX))
-    loads[3].wait()
-    pl.semaphore_wait(barrier, n_grp + 5)
-
-    pending = []
-
-    def send(src, dst, to, k):
-        c = pltpu.make_async_remote_copy(
-            src_ref=src, dst_ref=dst, send_sem=halo_send.at[k], recv_sem=halo_recv.at[k],
-            device_id=(to, grp), device_id_type=MESH)
-        c.start()
-        pending.append(c)
-        return c
-
-    cells = [send(rcs.at[3], rcs.at[3 - d], near[d], 27 + d) for d in near]
-    p0_down = send(p0_out, p0_in, below, 4)
-    w_up = send(w_out, w_in, above, 5)
-    b_up = send(b_out, b_in, above, 6)
-
+    near_out[2] = code((buoy - B_MID) * (TOP / B_MAX))
     for c in loads[4:7]:
         c.wait()
     e_dev = obs.shape[0]
@@ -145,16 +127,6 @@
     flat = obs[...].astype(F32).reshape(e_dev * steps, obs.shape[2]).astype(BF16)
     part = jnp.dot(lhs, flat, preferred_element_type=F32)
     encsend[...] = part.reshape(encsend.shape)
-    enc_copies = []
-    for d in range(1, n_grp):
-        peer = lax.rem(grp + d, n_grp)
-        c = pltpu.make_async_remote_copy(
-            src_ref=encsend.at[peer], dst_ref=encrecv.at[d], send_sem=enc_send.at[d],
-            recv_sem=enc_recv.at[d], device_id=(slab, peer), device_id_type=MESH)
-        c.start()
-        enc_copies.append(c)
-    pending += enc_copies
-
     loads[7].wait()
     wall = weights[...].astype(F32)
     shot_row = lax.broadcasted_iota(I32, wall.shape, 0)
@@ -168,6 +140,79 @@
     ax = jnp.where(row_e == ex, own, 0.0).astype(BF16)
     ay = jnp.where(row_e == (ec & 255), 1.0, 0.0).astype(BF16)
     amp = lax.dot_general(ax, ay, NT_DOT, preferred_element_type=F32)
+
+    xi = lax.broadcasted_iota(I32, (256, 256), 0)
+    yi = lax.broadcasted_iota(I32, (256, 256), 1)
+
+    def up_x(f):
+        return jnp.where(xi == 255, 0.0, pltpu.roll(f, 255, 0)) - f
+
+    def up_y(f):
+        return jnp.where(yi == 255, 0.0, pltpu.roll(f, 255, 1)) - f
+
+    def down_x(f):
+        return f - jnp.where(xi == 0, 0.0, pltpu.roll(f, 1, 0))
+
+    def down_y(f):
+        return f - jnp.where(yi == 0, 0.0, pltpu.roll(f, 1, 1))
+
+    has_above = slab < n_slab - 1
+    has_below = slab > 0
+    for c in loads[8:]:
+        c.wait()
+    kappa = dens[...] * speed[...] * speed[...]
+    keep = 1.0 - atten[...]
+    near_out[0] = code((kappa - K_MID) * (TOP / K_MAX))
+    near_out[1] = code((keep - D_MID) * (TOP / D_MAX))
+    hk = HALF * kappa
+    hb = HALF * buoy
+
+    def local_step(p, px, py):
+        px = px - hb * up_x(p)
+        py = py - hb * up_y(p)
+        return px, py, down_x(px) + down_y(py)
+
+    divs = [None] * steps
+    recorded = [None] * steps
+    p = press[0]
+    px, py, flat_div = local_step(p, vel[1], vel[2])
+    pz = vel[0] + hb * p
+    base = keep * p + wav[0] * amp
+    top = 1.001 * (
+        top_of(base - hk * (pz + flat_div)) + P_MAX * top_of(hk * hb) + V_MAX * top_of(hk))
+    p1_scale[...] = jnp.broadcast_to(top * (1.0 / TOP), (8, 128))
+    loads[3].wait()
+    pl.semaphore_wait(barrier, n_grp + 5)
+
+    pending = []
+
+    def send(src, dst, to, k):
+        c = pltpu.make_async_remote_copy(
+            src_ref=src, dst_ref=dst, send_sem=halo_send.at[k], recv_sem=halo_recv.at[k],
+            device_id=(to, grp), device_id_type=MESH)
+        c.start()
+        pending.append(c)
+        return c
+
+    cells = [send(rcs.at[3], rcs.at[3 - d], near[d], 27 + d) for d in near]
+    p0_down = send(p0_out, p0_in, below, 4)
+    w_up = send(w_out, w_in, above, 5)
+    b_up = send(near_out.at[2], b_in, above, 6)
+    quarter = pl.ds(pl.multiple_of(lax.rem(grp, 4) * 64, 64), 64)
+    pieces_in = [
+        send(near_out.at[:, quarter], near_in.at[0, :, quarter], below, 0),
+        send(near_out.at[0:2, quarter], near_in.at[1, 0:2, quarter], above, 1),
+        send(near_out.at[2, quarter], near_in.at[1, 2, quarter], near[2], 33)]
+
+    enc_copies = []
+    for d in range(1, n_grp):
+        peer = lax.rem(grp + d, n_grp)
+        c = pltpu.make_async_remote_copy(
+            src_ref=encsend.at[peer], dst_ref=encrecv.at[d], send_sem=enc_send.at[d],
+            recv_sem=enc_recv.at[d], device_id=(slab, peer), device_id_type=MESH)
+        c.start()
+        enc_copies.append(c)
+    pending += enc_copies
 
     for c in cells:
         c.wait_recv()
@@ -230,44 +275,6 @@
     count = scatter([ones] * 7, ring, plain)
     inv_ring = jnp.where(count > 0.5, 1.0 / count, 0.0)
 
-    xi = lax.broadcasted_iota(I32, (256, 256), 0)
-    yi = lax.broadcasted_iota(I32, (256, 256), 1)
-
-    def up_x(f):
-        return jnp.where(xi == 255, 0.0, pltpu.roll(f, 255, 0)) - f
-
-    def up_y(f):
-        return jnp.where(yi == 255, 0.0, pltpu.roll(f, 255, 1)) - f
-
-    def down_x(f):
-        return f - jnp.where(xi == 0, 0.0, pltpu.roll(f, 1, 0))
-
-    def down_y(f):
-        return f - jnp.where(yi == 0, 0.0, pltpu.roll(f, 1, 1))
-
-    has_above = slab < n_slab - 1
-    has_below = slab > 0
-    for c in loads[8:]:
-        c.wait()
-    kappa = dens[...] * speed[...] * speed[...]
-    keep = 1.0 - atten[...]
-    hk = HALF * kappa
-    hb = HALF * buoy
-
-    def local_step(p, px, py):
-        px = px - hb * up_x(p)
-        py = py - hb * up_y(p)
-        return px, py, down_x(px) + down_y(py)
-
-    divs = [None] * steps
-    recorded = [None] * steps
-    p = press[0]
-    px, py, flat_div = local_step(p, vel[1], vel[2])
-    pz = vel[0] + hb * p
-    base = keep * p + wav[0] * amp
-    top = 1.001 * (
-        top_of(base - hk * (pz + flat_div)) + P_MAX * top_of(hk * hb) + V_MAX * top_of(hk))
-    p1_scale[...] = jnp.broadcast_to(top * (1.0 / TOP), (8, 128))
     got = [
         send(p1_scale, p1_scale_in.at[0], below, 9), send(p1_scale, p1_scale_in.at[1], above, 10)]
     to_code = TOP / top
@@ -292,11 +299,6 @@
     p1_out[...] = code(p * to_code)
     got += [send(p1_out, p1_in.at[0], below, 7), send(p1_out, p1_in.at[1], above, 8)]
 
-    k_out[...] = code((kappa - K_MID) * (TOP / K_MAX))
-    d_out[...] = code((keep - D_MID) * (TOP / D_MAX))
-    planes = [
-        send(k_out, k_in.at[0], below, 0), send(k_out, k_in.at[1], above, 1),
-        send(d_out, d_in.at[0], below, 2), send(d_out, d_in.at[1], above, 3)]
     low_at = gather(split2(b_low), only + nearby)
     fix_out[...] = column([
         0.25 * kappa_at[5] * buoy_at[3], 0.25 * kappa_at[5] * low_at[1],
@@ -304,6 +306,18 @@
     fixed = [
         send(fix_out, fix_in.at[0], below, 11), send(fix_out, fix_in.at[1], above, 12),
         send(fix_out, fix2_in.at[0], near[-2], 31), send(fix_out, fix2_in.at[1], near[2], 32)]
+    for c in pieces_in:
+        c.wait_recv()
+    planes = []
+    for d in range(1, 4):
+        c = pltpu.make_async_remote_copy(
+            src_ref=near_in.at[:, :, quarter], dst_ref=near_in.at[:, :, quarter],
+            send_sem=halo_send.at[(2, 3, 34)[d - 1]], recv_sem=halo_recv.at[(2, 3, 34)[d - 1]],
+            device_id=(slab, lax.div(grp, 4) * 4 + lax.rem(lax.rem(grp, 4) + d, 4)),
+            device_id_type=MESH)
+        c.start()
+        planes.append(c)
+    pending += planes
     k_at, b_at = kappa_at[2], buoy_at[0]
     own_at = 0.25 * k_at * b_at
     star_at = [
@@ -337,7 +351,6 @@
     far = [
         send(far_out.at[0], far_in.at[0], near[-2], 15),
         send(far_out.at[1], far_in.at[1], near[2], 16)]
-    planes += [send(b_out, b2_in.at[0], below, 33), send(b_out, b2_in.at[1], near[2], 34)]
     px, py, flat_div = local_step(p, px, py)
     pz = pz + hb * p
     pzl = pzl - hbl * p
@@ -402,10 +415,10 @@
     base = inj[2] + keep * adj + spread(qb, total) - (qb + qbl) * total
     for c in planes:
         c.wait_recv()
-    k_near = [decode(k_in[i]) * (K_MAX / TOP) + K_MID for i in range(2)]
-    d_near = [decode(d_in[i]) * (D_MAX / TOP) + D_MID for i in range(2)]
+    k_near = [decode(near_in[i, 0]) * (K_MAX / TOP) + K_MID for i in range(2)]
+    d_near = [decode(near_in[i, 1]) * (D_MAX / TOP) + D_MID for i in range(2)]
     k_near[0] = jnp.where(has_above, k_near[0], 0.0)
-    b_near = [decode(b2_in[i]) * (B_MAX * 0.25 / TOP) + B_MID * 0.25 for i in range(2)]
+    b_near = [decode(near_in[i, 2]) * (B_MAX * 0.25 / TOP) + B_MID * 0.25 for i in range(2)]
     b_near[1] = jnp.where(slab > 1, b_near[1], 0.0)
     for c in got:
         c.wait_recv()
@@ -503,11 +516,10 @@
             pltpu.VMEM(weights.shape, BF16), pltpu.VMEM((1, emit), I32),
             pltpu.VMEM((1, emit), I32), pltpu.VMEM(observed.shape, BF16),
             pltpu.VMEM((7, 1, 128), I32),
-            plane(t=I16), plane(t=I16), plane(t=I16), plane(t=I16),
+            plane(t=I16), plane(t=I16), plane(t=I16),
             plane(t=I16), plane(t=I16), plane(t=I16), plane(2, t=I16),
             tile(), tile(2), tile(2), tile(2), tile(2), tile(2), tile(2), tile(2), tile(), tile(2),
-            tile(), tile(6), tile(2), plane(t=I16), plane(2, t=I16), plane(t=I16),
-            plane(2, t=I16), plane(2, t=I16),
+            tile(), tile(6), tile(2), plane(3, t=I16), plane(2, 3, t=I16),
             tile(n_grp), tile(n_grp), plane(2), plane(2, t=I16),
             pltpu.VMEM((n_grp, 2, rows, 256), I16), tile(2), tile(n_grp, 2),
             dma((10,)), dma((36,)), dma((36,)), dma((n_grp,)), dma((n_grp,)),

time: 58.7 us -> 56.6 us (0.964)
  Pallas kernels: 56.4 us -> 54.4 us
    pallas_call x1, Pallas kernels: 56.4 us -> 54.4 us  [shards(): pl.pallas_call(functools.partial(kernel, n_slab, n_grp), out_shape=out, i...]
where the time goes in v5:
time: 56.6 us; the launch traced here: 56.4 us
  Pallas kernels  54.4 us (96%)
  local copies, waits for them, and re-layouts  1.4 us (2%)
  between operations  0.64 us (1%)
    pallas_call x1, Pallas kernels, shards(): pl.pallas_call(functools.partial(kernel, n_slab, n_grp), out_shape=out, i...  54.4 us
    slice x1, local copies, waits for them, and re-layouts, shards(): return (both[0:1], both[1:2])  1.4 us

profile of v5, /device:TPU:6, one launch (start us, length us, event | category | flops | bytes accessed | tf_op | source)
XLA Modules:
  0.0 56.4 jit_solution(4859577975285094621)
XLA Ops:
  0.6 54.4 %shard_map.122 = f32[2,32,256]{2,1,0:T(8,128)} custom-call(f32[4]{0:T(128)} %wav.1, f32[1,256,256]{2,1,0:T(8,128)} %speed_h.1, f32[1,256,256]{2,1,0:T(8,128)} %dens_h.1, f32[1,256,256]{2,1,0:T(8,128)} %atten_h.1, f32[1,1,256,256]{3,2,1,0:T(8,128)} %press_h.1, f32[3,1,1,256,256]{4,3,2,1,0:T(8,128)} %vel_h.1, bf16[8,1024]{1,0:T(8,128)(2,1)} %weights_h.1, ...), custom_call_target="tpu_custom_call" | custom-call | tf_op jit(solution)/shard_map/pallas_call | solution.py:509
  55.0 1.4 %fusion = (f32[1,32,256]{2,1,0:T(8,128)}, f32[1,32,256]{2,1,0:T(8,128)}) fusion(f32[2,32,256]{2,1,0:T(8,128)} %shard_map.122), kind=kLoop, calls=%fused_computation | loop fusion | bytes 131072 | tf_op jit(solution)/shard_map/slice | solution.py:535

commit v6 on v5

--- a/solution.py
+++ b/solution.py
@@ -460,35 +460,38 @@
     gd = gd - adj * press[0]
     gk = gk - HALF * adj * divs[0]
     gk = gk * (2.0 * dens[...] * speed[...])
-    for i, g in enumerate((gk, gd)):
+    rows_out = 256 // n_grp
+    copies = {d: [] for d in range(1, n_grp)}
+
+    def to_peer(d, src, dst, sends, recvs):
+        c = pltpu.make_async_remote_copy(
+            src_ref=src, dst_ref=dst, send_sem=sends, recv_sem=recvs,
+            device_id=(slab, lax.rem(grp + d, n_grp)), device_id_type=MESH)
+        c.start()
+        copies[d].append(c)
+
+    for i, g in ((1, gd), (0, gk)):
         grad[i] = g
         top = jnp.maximum(top_of(g), 1e-30)
         coded[i] = code_root(g, top)
         gscale[i] = jnp.broadcast_to(top * (1.0 / (TOP * TOP)), (8, 128))
-    rows_out = 256 // n_grp
-    copies = []
+        for d in range(1, n_grp):
+            start = lax.rem(grp + d, n_grp) * rows_out
+            to_peer(
+                d, coded.at[i, pl.ds(pl.multiple_of(start, rows_out), rows_out)],
+                gradrecv.at[d, i], grad_send.at[i, d], grad_recv.at[i, d])
     for d in range(1, n_grp):
-        peer = lax.rem(grp + d, n_grp)
-        c = pltpu.make_async_remote_copy(
-            src_ref=coded.at[:, pl.ds(pl.multiple_of(peer * rows_out, rows_out), rows_out)],
-            dst_ref=gradrecv.at[d], send_sem=grad_send.at[d],
-            recv_sem=grad_recv.at[d], device_id=(slab, peer), device_id_type=MESH)
-        c.start()
-        e = pltpu.make_async_remote_copy(
-            src_ref=gscale, dst_ref=gscale_in.at[d], send_sem=gs_send.at[d],
-            recv_sem=gs_recv.at[d], device_id=(slab, peer), device_id_type=MESH)
-        e.start()
-        copies.append((c, e))
+        to_peer(d, gscale, gscale_in.at[d], gs_send.at[d], gs_recv.at[d])
     mine = pl.ds(pl.multiple_of(grp * rows_out, rows_out), rows_out)
     total = [grad[0, mine], grad[1, mine]]
     for d in range(1, n_grp):
-        for c in copies[d - 1]:
+        for c in copies[d]:
             c.wait_recv()
         for i in range(2):
             total[i] = total[i] + decode_root(gradrecv[d, i]) * gscale_in[d, i, 0:1, 0:1]
     out[0] = total[0]
     out[1] = total[1]
-    for c in pending + [c for pair in copies for c in pair]:
+    for c in pending + [c for d in copies for c in copies[d]]:
         c.wait_send()
 
 
@@ -523,7 +526,7 @@
             tile(n_grp), tile(n_grp), plane(2), plane(2, t=I16),
             pltpu.VMEM((n_grp, 2, rows, 256), I16), tile(2), tile(n_grp, 2),
             dma((10,)), dma((36,)), dma((36,)), dma((n_grp,)), dma((n_grp,)),
-            dma((n_grp,)), dma((n_grp,)), dma((n_grp,)), dma((n_grp,)),
+            dma((2, n_grp)), dma((2, n_grp)), dma((n_grp,)), dma((n_grp,)),
         ],
         compiler_params=pltpu.CompilerParams(
             collective_id=0, has_side_effects=True, vmem_limit_bytes=60 * 1024 * 1024),

time: 56.6 us -> 57.7 us (1.019)
  the two profiles are of different devices: /device:TPU:6 before, /device:TPU:1 now
where the time goes in v6:
time: 57.7 us; the launch traced here: 57.5 us
  Pallas kernels  55.4 us (96%)
  local copies, waits for them, and re-layouts  1.4 us (2%)
  between operations  0.64 us (1%)
    pallas_call x1, Pallas kernels, shards(): pl.pallas_call(functools.partial(kernel, n_slab, n_grp), out_shape=out, i...  55.4 us
    slice x1, local copies, waits for them, and re-layouts, shards(): return (both[0:1], both[1:2])  1.4 us

profile of v6, /device:TPU:1, one launch (start us, length us, event | category | flops | bytes accessed | tf_op | source)
XLA Modules:
  0.0 57.5 jit_solution(14684843740458637024)
XLA Ops:
  0.6 55.4 %shard_map.122 = f32[2,32,256]{2,1,0:T(8,128)} custom-call(f32[4]{0:T(128)} %wav.1, f32[1,256,256]{2,1,0:T(8,128)} %speed_h.1, f32[1,256,256]{2,1,0:T(8,128)} %dens_h.1, f32[1,256,256]{2,1,0:T(8,128)} %atten_h.1, f32[1,1,256,256]{3,2,1,0:T(8,128)} %press_h.1, f32[3,1,1,256,256]{4,3,2,1,0:T(8,128)} %vel_h.1, bf16[8,1024]{1,0:T(8,128)(2,1)} %weights_h.1, ...), custom_call_target="tpu_custom_call" | custom-call | tf_op jit(solution)/shard_map/pallas_call | solution.py:512
  56.1 1.4 %fusion = (f32[1,32,256]{2,1,0:T(8,128)}, f32[1,32,256]{2,1,0:T(8,128)}) fusion(f32[2,32,256]{2,1,0:T(8,128)} %shard_map.122), kind=kLoop, calls=%fused_computation | loop fusion | bytes 131072 | tf_op jit(solution)/shard_map/slice | solution.py:538
